TPU v7x, 32 devices: a whole 2x2x4 slice. The times are simulated.
32 devices in a mesh: pipe: 4 (over x, core), dp: 8 (over z, y).
Axes of the slice: x: 2, y: 2, z: 4, core: 2. Of those that a mesh axis runs over, the one named last changes fastest.
Arguments:
- lookback_readings: bfloat16 [4, 4096, 336], P('pipe', 'dp'), may hold values from -6 to 6
- prediction_adjoint: bfloat16 [4, 4096, 96], P('pipe', 'dp'), may hold values from -6 to 6
- variate_tallies: int32 [4, 8, 4], P(None, 'dp'), may hold values from 1 to 321, 512 in all within a row
- lookback_classes: int32 [4, 8, 4], P(None, 'dp'), may hold values from 0 to 2
- brief_lift_table: bfloat16 [96, 512], replicated, may hold values from -0.625 to 0.625
- moderate_lift_table: bfloat16 [192, 512], replicated, may hold values from -0.4375 to 0.4375
- distant_lift_table: bfloat16 [336, 512], replicated, may hold values from -0.3125 to 0.3125
- lift_offsets: float32 [3, 512], replicated, may hold values from -3 to 3
- part_entry_arrays: bfloat16 [4, 512, 2048], P('pipe'), may hold values from -3 to 3
- part_shrink_lines: bfloat16 [4, 1024, 512], P('pipe'), may hold values from -0.125 to 0.125
- part_layernorm_scale: float32 [4, 512], P('pipe'), may hold values from 0.5 to 1.5
- part_layernorm_offset: float32 [4, 512], P('pipe'), may hold values from -2 to 2
- mixing_offsets: float32 [2, 3, 512], replicated, may hold values from -2 to 2
- expand_offsets: float32 [2, 2048], replicated, may hold values from -2 to 2
- shrink_offsets: float32 [2, 512], replicated, may hold values from -2 to 2
- prediction_matrix: bfloat16 [512, 96], replicated, may hold values from -0.25 to 0.25
- prediction_offset: float32 [96], replicated, may hold values from -3 to 3
Outputs:
- prediction: bfloat16 [4, 4096, 96], P('pipe', 'dp')
- series_grad: float32 [4, 4096, 336], P('pipe', 'dp')
- emb_short_grad: float32 [96, 512], replicated
- emb_mid_grad: float32 [192, 512], replicated
- emb_long_grad: float32 [336, 512], replicated
- emb_bias_grad: float32 [3, 512], replicated
- section_in_grad: float32 [4, 512, 2048], P('pipe')
- section_down_grad: float32 [4, 1024, 512], P('pipe')
- norm_gain_grad: float32 [4, 512], P('pipe')
- norm_bias_grad: float32 [4, 512], P('pipe')
- att_bias_grad: float32 [2, 3, 512], replicated
- up_bias_grad: float32 [2, 2048], replicated
- down_bias_grad: float32 [2, 512], replicated
- proj_w_grad: float32 [512, 96], replicated
- proj_b_grad: float32 [96], replicated
Inputs may be any that keep to these rules, and one draw needn't show every extreme that they name: `variate_tallies`: each row's 4 window sizes sum to 512, and in every row the largest is 321.
All inputs are finite; a program needn't handle non-finite values.
Results may differ from a plain program's by a relative error of at most 0.023.
Values may be sent and summed in bfloat16 or wider, within the bound.
No kernel may reach another device: no remote copies, remote signals or barrier semaphores. Data moves between devices by JAX's collectives and lax.ppermute only.
A program may use at most 384 MiB of HBM per device.

v0:
```python
import jax
import jax.numpy as jnp
from jax import lax
from jax.sharding import PartitionSpec as P

HEADS = 8
HEAD_DIM = 64


def shifted(array, axis, by):
    devices = lax.axis_size(axis)
    pairs = [(i, i + by) for i in range(devices) if 0 <= i + by < devices]
    return lax.ppermute(array, axis, pairs)


def as_sent(array):
    return jax.tree.map(lambda a: a.astype(jnp.bfloat16) if a.dtype == jnp.float32 else a, array)


def layer_norm_parts(summed, norm_gain_row, norm_offset):
    centre = summed - jnp.mean(summed, -1, keepdims=True)
    spread = jnp.mean(centre * centre, -1, keepdims=True)
    inverse = lax.rsqrt(spread + 1e-05)
    normed = centre * inverse
    return (normed * norm_gain_row + norm_offset, normed, inverse)


def layer_norm_back(upstream, normed, inverse, norm_gain_row):
    gain_grad = jnp.sum(upstream * normed, 0)
    offset_grad = jnp.sum(upstream, 0)
    scaled = upstream * norm_gain_row
    centred_grad = (
        scaled
        - jnp.mean(scaled, -1, keepdims=True)
        - normed * jnp.mean(scaled * normed, -1, keepdims=True)
    )
    return (centred_grad * inverse, gain_grad, offset_grad)


def row_layout(variate_tallies, lookback_classes, row_len):
    window_end = jnp.cumsum(variate_tallies, -1)
    position = jnp.arange(row_len, dtype=jnp.int32)
    packed_fragment = jnp.sum(
        (position[None, :, None] >= window_end[:, None, :]).astype(jnp.int32), -1
    )
    windows = jnp.arange(variate_tallies.shape[-1], dtype=jnp.int32)
    picked = jnp.sum(
        jnp.where(
            packed_fragment[:, :, None] == windows[None, None, :], lookback_classes[:, None, :], 0
        ),
        -1,
    )
    return (packed_fragment, picked)


def gelu_exact(inputs):
    return jax.nn.gelu(inputs, approximate=False)


def attention_forward(inputs_bf, matrix, biases, norm_gain_row, norm_offset, packed_fragment):
    model_width = inputs_bf.shape[1]
    project = jnp.dot(inputs_bf, matrix[:, : 3 * model_width], preferred_element_type=jnp.float32)
    head_shape = (packed_fragment.shape[0], packed_fragment.shape[1], HEADS, HEAD_DIM)
    query_heads = (project[:, :model_width] + biases[0]).astype(jnp.bfloat16).reshape(head_shape)
    key_heads = project[:, model_width : 2 * model_width].astype(jnp.bfloat16).reshape(head_shape)
    value_heads = (
        (project[:, 2 * model_width :] + biases[1]).astype(jnp.bfloat16).reshape(head_shape)
    )
    scores = jnp.einsum(
        "rqhd,rkhd->rhqk", query_heads, key_heads, preferred_element_type=jnp.float32
    ) * HEAD_DIM ** (-0.5)
    same_window = (packed_fragment[:, :, None] == packed_fragment[:, None, :])[:, None]
    scores = jnp.where(same_window, scores, -1e30)
    row_max = jnp.max(scores, -1, keepdims=True)
    weights = jnp.exp(scores - row_max)
    weights = weights / jnp.sum(weights, -1, keepdims=True)
    weights_bf = weights.astype(jnp.bfloat16)
    mixture = jnp.einsum(
        "rhqk,rkhd->rqhd", weights_bf, value_heads, preferred_element_type=jnp.float32
    )
    mixture_bf = mixture.reshape(-1, model_width).astype(jnp.bfloat16)
    branch = (
        jnp.dot(mixture_bf, matrix[:, 3 * model_width :], preferred_element_type=jnp.float32)
        + biases[2]
    )
    output, normed, inverse = layer_norm_parts(
        inputs_bf.astype(jnp.float32) + branch, norm_gain_row, norm_offset
    )
    return (
        output,
        (query_heads, key_heads, value_heads, weights, weights_bf, mixture_bf, normed, inverse),
    )


def attention_backward(upstream, inputs_bf, matrix, norm_gain_row, saved_parts):
    query_heads, key_heads, value_heads, weights, weights_bf, mixture_bf, normed, inverse = (
        saved_parts
    )
    model_width = inputs_bf.shape[1]
    summed_grad, gain_grad, offset_grad = layer_norm_back(upstream, normed, inverse, norm_gain_row)
    branch_bf = summed_grad.astype(jnp.bfloat16)
    out_matrix_grad = jnp.dot(mixture_bf.T, branch_bf, preferred_element_type=jnp.float32)
    out_bias_grad = jnp.sum(branch_bf.astype(jnp.float32), 0)
    mixture_grad = jnp.dot(
        branch_bf, matrix[:, 3 * model_width :].T, preferred_element_type=jnp.float32
    )
    mixture_grad = mixture_grad.astype(jnp.bfloat16).reshape(query_heads.shape)
    weight_grad = jnp.einsum(
        "rqhd,rkhd->rhqk", mixture_grad, value_heads, preferred_element_type=jnp.float32
    )
    value_grad = jnp.einsum(
        "rhqk,rqhd->rkhd", weights_bf, mixture_grad, preferred_element_type=jnp.float32
    )
    centred = jnp.sum(weights * weight_grad, -1, keepdims=True)
    score_grad = (weights * (weight_grad - centred)).astype(jnp.bfloat16)
    query_grad = jnp.einsum(
        "rhqk,rkhd->rqhd", score_grad, key_heads, preferred_element_type=jnp.float32
    ) * HEAD_DIM ** (-0.5)
    key_grad = jnp.einsum(
        "rhqk,rqhd->rkhd", score_grad, query_heads, preferred_element_type=jnp.float32
    ) * HEAD_DIM ** (-0.5)
    project_grad = jnp.concatenate(
        [
            query_grad.reshape(-1, model_width),
            key_grad.reshape(-1, model_width),
            value_grad.reshape(-1, model_width),
        ],
        1,
    ).astype(jnp.bfloat16)
    in_matrix_grad = jnp.dot(inputs_bf.T, project_grad, preferred_element_type=jnp.float32)
    project_float = project_grad.astype(jnp.float32)
    query_bias_grad = jnp.sum(project_float[:, :model_width], 0)
    value_bias_grad = jnp.sum(project_float[:, 2 * model_width :], 0)
    input_grad = summed_grad + jnp.dot(
        project_grad, matrix[:, : 3 * model_width].T, preferred_element_type=jnp.float32
    )
    matrix_grad = jnp.concatenate([in_matrix_grad, out_matrix_grad], 1)
    bias_grad = jnp.stack([query_bias_grad, value_bias_grad, out_bias_grad])
    return (input_grad, matrix_grad, bias_grad, gain_grad, offset_grad)


def feed_forward(
    inputs_bf, up_matrix, down_matrix, up_offset, down_offset, norm_gain_row, norm_offset
):
    hidden_pre = jnp.dot(inputs_bf, up_matrix, preferred_element_type=jnp.float32) + up_offset
    hidden_bf = gelu_exact(hidden_pre).astype(jnp.bfloat16)
    branch = jnp.dot(hidden_bf, down_matrix, preferred_element_type=jnp.float32) + down_offset
    output, normed, inverse = layer_norm_parts(
        inputs_bf.astype(jnp.float32) + branch, norm_gain_row, norm_offset
    )
    return (output, (hidden_pre, hidden_bf, normed, inverse))


def feed_backward(upstream, inputs_bf, up_matrix, down_matrix, norm_gain_row, saved_parts):
    hidden_pre, hidden_bf, normed, inverse = saved_parts
    summed_grad, gain_grad, offset_grad = layer_norm_back(upstream, normed, inverse, norm_gain_row)
    branch_bf = summed_grad.astype(jnp.bfloat16)
    down_grad = jnp.dot(hidden_bf.T, branch_bf, preferred_element_type=jnp.float32)
    down_offset_grad = jnp.sum(branch_bf.astype(jnp.float32), 0)
    hidden_grad = jnp.dot(branch_bf, down_matrix.T, preferred_element_type=jnp.float32)
    activated, gelu_pull = jax.vjp(gelu_exact, hidden_pre)
    pre_bf = gelu_pull(hidden_grad)[0].astype(jnp.bfloat16)
    up_grad = jnp.dot(inputs_bf.T, pre_bf, preferred_element_type=jnp.float32)
    up_offset_grad = jnp.sum(pre_bf.astype(jnp.float32), 0)
    input_grad = summed_grad + jnp.dot(pre_bf, up_matrix.T, preferred_element_type=jnp.float32)
    return (
        input_grad,
        up_grad,
        down_grad,
        up_offset_grad,
        down_offset_grad,
        gain_grad,
        offset_grad,
    )


def embed_forward(tokens_bf, variate_class, tables, lift_offsets):
    look_width = tokens_bf.shape[1]
    result = jnp.zeros((tokens_bf.shape[0], lift_offsets.shape[1]), jnp.float32)
    for group_index in range(3):
        emb_table = tables[group_index]
        lookback = emb_table.shape[0]
        chosen = (variate_class == group_index).astype(jnp.float32)[:, None]
        result = result + chosen * (
            jnp.dot(
                tokens_bf[:, look_width - lookback :], emb_table, preferred_element_type=jnp.float32
            )
            + lift_offsets[group_index]
        )
    return result


def embed_backward(embed_grad_bf, tokens_bf, variate_class, tables):
    look_width = tokens_bf.shape[1]
    table_grads = []
    bias_grads = []
    series_piece = jnp.zeros(tokens_bf.shape, jnp.float32)
    for group_index in range(3):
        emb_table = tables[group_index]
        lookback = emb_table.shape[0]
        start_col = look_width - lookback
        chosen = (variate_class == group_index).astype(jnp.bfloat16)[:, None]
        masked = embed_grad_bf * chosen
        table_grads.append(
            jnp.dot(tokens_bf[:, start_col:].T, masked, preferred_element_type=jnp.float32)
        )
        bias_grads.append(jnp.sum(masked.astype(jnp.float32), 0))
        spread_back = jnp.dot(masked, emb_table.T, preferred_element_type=jnp.float32)
        series_piece = series_piece + jnp.pad(spread_back, ((0, 0), (start_col, 0)))
    return (table_grads, jnp.stack(bias_grads), series_piece)


def place_layer(piece, layer_index):
    stacked = [jnp.zeros_like(piece), jnp.zeros_like(piece)]
    stacked[layer_index] = piece
    return jnp.stack(stacked)


def per_device(
    lookback_readings,
    prediction_adjoint,
    variate_tallies,
    lookback_classes,
    brief_lift_table,
    moderate_lift_table,
    distant_lift_table,
    lift_offsets,
    part_entry_arrays,
    part_shrink_lines,
    part_layernorm_scale,
    part_layernorm_offset,
    mixing_offsets,
    expand_offsets,
    shrink_offsets,
    prediction_matrix,
    prediction_offset,
):
    part_place = lax.axis_index("pipe")
    part_tally = lax.axis_size("pipe")
    all_series, all_cotangent = (
        lax.all_gather(lookback_readings, "pipe", axis=0, tiled=True),
        lax.all_gather(prediction_adjoint, "pipe", axis=0, tiled=True),
    )
    subgroup_number = all_series.shape[0]
    variate_tally = all_series.shape[1]
    model_width = part_entry_arrays.shape[1]
    half_rows = part_shrink_lines.shape[1]
    emitted_breadth = prediction_matrix.shape[1]
    rows_mb = variate_tallies.shape[1]
    row_len = variate_tally // rows_mb
    packed_fragment, picked = row_layout(
        variate_tallies.reshape(-1, variate_tallies.shape[2]),
        lookback_classes.reshape(-1, lookback_classes.shape[2]),
        row_len,
    )
    packed_fragment = packed_fragment.reshape(subgroup_number, rows_mb, row_len)
    in_matrix = part_entry_arrays[0]
    own_down = part_shrink_lines[0]
    prior_down = shifted(own_down, "pipe", 1)
    down_matrix = jnp.concatenate([prior_down, own_down], 0)
    section_gain = part_layernorm_scale[0]
    section_offset = part_layernorm_offset[0]
    tables = (brief_lift_table, moderate_lift_table, distant_lift_table)
    grad_shapes = (
        in_matrix.shape,
        (2 * half_rows, model_width),
        (model_width,),
        (model_width,),
        brief_lift_table.shape,
        moderate_lift_table.shape,
        distant_lift_table.shape,
        lift_offsets.shape,
        mixing_offsets.shape,
        expand_offsets.shape,
        shrink_offsets.shape,
        prediction_matrix.shape,
        prediction_offset.shape,
    )

    def zero_set():
        return [jnp.zeros(shape_now, jnp.float32) for shape_now in grad_shapes]

    def section_forward(section_id, received_now, slot_now):
        if section_id == 0:
            tokens_bf = lax.dynamic_index_in_dim(all_series, slot_now, 0, False)
            group_now = lax.dynamic_index_in_dim(picked, slot_now, 0, False)
            inputs_bf = embed_forward(tokens_bf, group_now, tables, lift_offsets).astype(
                jnp.bfloat16
            )
        else:
            inputs_bf = received_now
        layer_index = section_id // 2
        if section_id % 2 == 0:
            segment_now = lax.dynamic_index_in_dim(packed_fragment, slot_now, 0, False)
            output, saved_parts = attention_forward(
                inputs_bf,
                in_matrix,
                mixing_offsets[layer_index],
                section_gain,
                section_offset,
                segment_now,
            )
        else:
            output, saved_parts = feed_forward(
                inputs_bf,
                in_matrix,
                down_matrix,
                expand_offsets[layer_index],
                shrink_offsets[layer_index],
                section_gain,
                section_offset,
            )
        return (inputs_bf, output, saved_parts)

    def forward_branch(section_id):

        def forward_section_run(received_now, slot_now):
            inputs_bf, output, saved_parts = section_forward(section_id, received_now, slot_now)
            emitted_halfprec = output.astype(jnp.bfloat16)
            if section_id == part_tally - 1:
                prediction = (
                    jnp.dot(emitted_halfprec, prediction_matrix, preferred_element_type=jnp.float32)
                    + prediction_offset
                )
            else:
                prediction = jnp.zeros((variate_tally, emitted_breadth), jnp.float32)
            return (emitted_halfprec, prediction)

        return forward_section_run

    def backward_branch(section_id):

        def backward_section_run(upstream_bf, slot_now):
            received_now = lax.dynamic_index_in_dim(kept_inputs, slot_now, 0, False)
            inputs_bf, output, saved_parts = section_forward(section_id, received_now, slot_now)
            layer_index = section_id // 2
            derivative_collection = zero_set()
            if section_id == part_tally - 1:
                adjoint_halfprec = lax.dynamic_index_in_dim(all_cotangent, slot_now, 0, False)
                emitted_halfprec = output.astype(jnp.bfloat16)
                derivative_collection[11] = jnp.dot(
                    emitted_halfprec.T, adjoint_halfprec, preferred_element_type=jnp.float32
                )
                derivative_collection[12] = jnp.sum(adjoint_halfprec.astype(jnp.float32), 0)
                upstream = jnp.dot(
                    adjoint_halfprec, prediction_matrix.T, preferred_element_type=jnp.float32
                )
            else:
                upstream = upstream_bf.astype(jnp.float32)
            if section_id % 2 == 0:
                input_grad, matrix_grad, bias_grad, gain_grad, offset_grad = attention_backward(
                    upstream, inputs_bf, in_matrix, section_gain, saved_parts
                )
                derivative_collection[0] = matrix_grad
                derivative_collection[8] = place_layer(bias_grad, layer_index)
            else:
                (
                    input_grad,
                    up_grad,
                    down_grad,
                    up_offset_grad,
                    down_offset_grad,
                    gain_grad,
                    offset_grad,
                ) = feed_backward(
                    upstream, inputs_bf, in_matrix, down_matrix, section_gain, saved_parts
                )
                derivative_collection[0] = up_grad
                derivative_collection[1] = down_grad
                derivative_collection[9] = place_layer(up_offset_grad, layer_index)
                derivative_collection[10] = place_layer(down_offset_grad, layer_index)
            derivative_collection[2] = gain_grad
            derivative_collection[3] = offset_grad
            input_grad_bf = input_grad.astype(jnp.bfloat16)
            series_piece = jnp.zeros((variate_tally, all_series.shape[2]), jnp.float32)
            if section_id == 0:
                tokens_bf = lax.dynamic_index_in_dim(all_series, slot_now, 0, False)
                group_now = lax.dynamic_index_in_dim(picked, slot_now, 0, False)
                table_grads, bias_stack, series_piece = embed_backward(
                    input_grad_bf, tokens_bf, group_now, tables
                )
                derivative_collection[4] = table_grads[0]
                derivative_collection[5] = table_grads[1]
                derivative_collection[6] = table_grads[2]
                derivative_collection[7] = bias_stack
            return (input_grad_bf, tuple(derivative_collection), series_piece)

        return backward_section_run

    forward_runs = [forward_branch(section_id) for section_id in range(part_tally)]
    backward_runs = [backward_branch(section_id) for section_id in range(part_tally)]

    def forward_selector(received_now, slot_now):
        return lax.switch(part_place, forward_runs, received_now, slot_now)

    def forward_bypass(received_now, slot_now):
        return (
            jnp.zeros_like(received_now),
            jnp.zeros((variate_tally, emitted_breadth), jnp.float32),
        )

    def backward_switch(upstream_bf, slot_now):
        return lax.switch(part_place, backward_runs, upstream_bf, slot_now)

    def skip_backward(upstream_bf, slot_now):
        return (
            jnp.zeros_like(upstream_bf),
            tuple(zero_set()),
            jnp.zeros((variate_tally, all_series.shape[2]), jnp.float32),
        )

    received_state = jnp.zeros((variate_tally, model_width), jnp.bfloat16)
    kept_inputs = jnp.zeros((subgroup_number, variate_tally, model_width), jnp.bfloat16)
    prediction_lines = jnp.zeros((subgroup_number, variate_tally, emitted_breadth), jnp.float32)
    for moment in range(subgroup_number + part_tally - 1):
        micro_index = moment - part_place
        active_flag = (micro_index >= 0) & (micro_index < subgroup_number)
        place_index = jnp.clip(micro_index, 0, subgroup_number - 1)
        kept_inputs = jnp.where(
            active_flag,
            lax.dynamic_update_index_in_dim(kept_inputs, received_state, place_index, 0),
            kept_inputs,
        )
        outgoing_activation, prediction = lax.cond(
            active_flag, forward_selector, forward_bypass, received_state, place_index
        )
        prediction_lines = jnp.where(
            active_flag,
            lax.dynamic_update_index_in_dim(prediction_lines, prediction, place_index, 0),
            prediction_lines,
        )
        received_state = jax.tree.map(
            lambda part, own: part.astype(own.dtype),
            shifted(as_sent(outgoing_activation), "pipe", 1),
            outgoing_activation,
        )
    upstream_now = jnp.zeros((variate_tally, model_width), jnp.bfloat16)
    totals = tuple(zero_set())
    series_total = jnp.zeros(all_series.shape, jnp.float32)
    for moment in range(subgroup_number + part_tally - 1):
        micro_index = moment - (part_tally - 1 - part_place)
        active_flag = (micro_index >= 0) & (micro_index < subgroup_number)
        place_index = jnp.clip(micro_index, 0, subgroup_number - 1)
        outgoing_activation, increments, series_piece = lax.cond(
            active_flag, backward_switch, skip_backward, upstream_now, place_index
        )
        totals = tuple((total + increment for total, increment in zip(totals, increments)))
        series_total = lax.dynamic_update_index_in_dim(
            series_total,
            lax.dynamic_index_in_dim(series_total, place_index, 0, False) + series_piece,
            place_index,
            0,
        )
        upstream_now = jax.tree.map(
            lambda part, own: part.astype(own.dtype),
            shifted(as_sent(outgoing_activation), "pipe", -1),
            outgoing_activation,
        )
    even_section = part_place % 2 == 0
    returned = shifted(as_sent(totals[1][:half_rows]), "pipe", -1)
    down_local = jnp.where(even_section, returned, totals[1][half_rows:])
    in_sum, down_mine, gain_sum, offset_sum = lax.psum(
        (totals[0], down_local, totals[2], totals[3]), "dp"
    )
    shared = lax.psum(
        (
            totals[4],
            totals[5],
            totals[6],
            totals[7],
            totals[8],
            totals[9],
            totals[10],
            totals[11],
            totals[12],
        ),
        ("pipe", "dp"),
    )
    prediction_portion = jnp.where(part_place == part_tally - 1, prediction_lines, 0.0)
    series_part = jnp.where(part_place == 0, series_total, 0.0)
    prediction_outcome, readings_emitted = (
        lax.psum_scatter(
            prediction_portion.astype(jnp.bfloat16), "pipe", scatter_dimension=0, tiled=True
        ).astype(jnp.float32),
        lax.psum_scatter(
            series_part.astype(jnp.bfloat16), "pipe", scatter_dimension=0, tiled=True
        ).astype(jnp.float32),
    )
    return (
        prediction_outcome.astype(jnp.bfloat16),
        readings_emitted,
        shared[0],
        shared[1],
        shared[2],
        shared[3],
        in_sum[None],
        down_mine[None],
        gain_sum[None],
        offset_sum[None],
        shared[4],
        shared[5],
        shared[6],
        shared[7],
        shared[8],
    )


def solution(mesh):
    placed = (
        P("pipe", "dp", None),
        P("pipe", "dp", None),
        P(None, "dp", None),
        P(None, "dp", None),
        P(),
        P(),
        P(),
        P(),
        P("pipe", None, None),
        P("pipe", None, None),
        P("pipe", None),
        P("pipe", None),
        P(),
        P(),
        P(),
        P(),
        P(),
    )
    return jax.shard_map(
        per_device,
        mesh=mesh,
        in_specs=placed,
        out_specs=(
            P("pipe", "dp", None),
            P("pipe", "dp", None),
            P(),
            P(),
            P(),
            P(),
            P("pipe", None, None),
            P("pipe", None, None),
            P("pipe", None),
            P("pipe", None),
            P(),
            P(),
            P(),
            P(),
            P(),
        ),
        check_vma=False,
    )
```

profile of v0, /device:TPU:0, one launch (start us, length us, event | category | flops | bytes accessed | tf_op | source)
XLA Modules:
  0.0 1411.9 jit_solution(4168942232385896226)
XLA Ops:
  16.3 14.9 %all-gather.2.cloned.1.call-done = bf16[4,512,336]{1,2,0:T(8,128)(2,1)} async-done(((bf16[1,512,336]{1,2,0:T(8,128)(2,1)}), bf16[4,512,336]{1,2,0:T(8,128)(2,1)}) %all-gather.2.cloned.1.call-update) | async-done | bytes 1376272 | tf_op jit(solution)/shard_map/all_gather | solution.py:241
  31.3 52.5 %conditional.94 = (bf16[512,512]{0,1:T(8,128)(2,1)}, bf16[1,512,96]{1,2,0:T(8,128)(2,1)}) conditional(s32[]{:T(128)} %convert_element_type.2350, () %tuple.597, (s32[]{:T(128)}, s32[]{:T(128)}, s32[4,512]{1,0:T(4,128)S(1)}, bf16[4,512,336]{1,2,0:T(8,128)(2,1)}, bf16[96,512]{1,0:T(8,128)(2,1)S(1)}, /*index=5*/f32[3,512]{1,0:T(4,128)S(1)}, ...), branch_computations={%region_3.4_spmd, %region_4.21_spmd} | conditional | flops 2269741568 | bytes 63789492 | solution.py:424
  31.4 46.1 %conditional.128 = (bf16[1,512,96]{1,2,0:T(8,128)(2,1)}, bf16[512,512]{0,1:T(8,128)(2,1)}) conditional(s32[]{:T(128)} %clamp.28, (s32[]{:T(128)}, s32[4,512]{1,0:T(4,128)S(1)}, bf16[4,512,336]{1,2,0:T(8,128)(2,1)}, bf16[96,512]{1,0:T(8,128)(2,1)S(1)}, f32[3,512]{1,0:T(4,128)S(1)}, ...), branch_computations={%region_5.9_spmd, %region_10.12_spmd, %region_13.17_spmd, %region_... | conditional | flops 2269741568 | bytes 63748244
  89.0 54.8 %conditional.95 = (bf16[512,512]{0,1:T(8,128)(2,1)}, bf16[1,512,96]{1,2,0:T(8,128)(2,1)}) conditional(s32[]{:T(128)} %convert_element_type.2352, () %tuple.599, (s32[]{:T(128)}, s32[]{:T(128)}, s32[4,512]{1,0:T(4,128)S(1)}, bf16[4,512,336]{1,2,0:T(8,128)(2,1)}, bf16[96,512]{1,0:T(8,128)(2,1)S(1)}, /*index=5*/f32[3,512]{1,0:T(4,128)S(1)}, ...), branch_computations={%region_21.22_spmd, %region_22.39_spmd} | conditional | flops 2270265856 | bytes 64838092 | solution.py:424
  91.1 46.2 %conditional.129 = (bf16[1,512,96]{1,2,0:T(8,128)(2,1)}, bf16[512,512]{0,1:T(8,128)(2,1)}) conditional(s32[]{:T(128)} %clamp.29, (s32[]{:T(128)}, s32[4,512]{1,0:T(4,128)S(1)}, bf16[4,512,336]{1,2,0:T(8,128)(2,1)}, bf16[96,512]{1,0:T(8,128)(2,1)S(1)}, f32[3,512]{1,0:T(4,128)S(1)}, ...), branch_computations={%region_23.27_spmd, %region_28.30_spmd, %region_31.35_spmd, %regio... | conditional | flops 2270265856 | bytes 63748244
  149.1 54.5 %conditional.96 = (bf16[512,512]{0,1:T(8,128)(2,1)}, bf16[1,512,96]{1,2,0:T(8,128)(2,1)}) conditional(s32[]{:T(128)} %convert_element_type.2353, () %tuple.601, (s32[]{:T(128)}, s32[]{:T(128)}, s32[4,512]{1,0:T(4,128)S(1)}, bf16[4,512,336]{1,2,0:T(8,128)(2,1)}, bf16[96,512]{1,0:T(8,128)(2,1)S(1)}, /*index=5*/f32[3,512]{1,0:T(4,128)S(1)}, ...), branch_computations={%region_39.40_spmd, %region_40.57_spmd} | conditional | flops 2270265856 | bytes 64838092 | solution.py:424
  151.1 46.2 %conditional.130 = (bf16[1,512,96]{1,2,0:T(8,128)(2,1)}, bf16[512,512]{0,1:T(8,128)(2,1)}) conditional(s32[]{:T(128)} %clamp.30, (s32[]{:T(128)}, s32[4,512]{1,0:T(4,128)S(1)}, bf16[4,512,336]{1,2,0:T(8,128)(2,1)}, bf16[96,512]{1,0:T(8,128)(2,1)S(1)}, f32[3,512]{1,0:T(4,128)S(1)}, ...), branch_computations={%region_41.45_spmd, %region_46.48_spmd, %region_49.53_spmd, %regio... | conditional | flops 2270265856 | bytes 63748244
  208.8 54.0 %conditional.97 = (bf16[512,512]{0,1:T(8,128)(2,1)}, bf16[1,512,96]{1,2,0:T(8,128)(2,1)}) conditional(s32[]{:T(128)} %convert_element_type.2354, () %tuple.603, (s32[]{:T(128)}, s32[]{:T(128)}, s32[4,512]{1,0:T(4,128)S(1)}, bf16[4,512,336]{1,2,0:T(8,128)(2,1)}, bf16[96,512]{1,0:T(8,128)(2,1)S(1)}, /*index=5*/f32[3,512]{1,0:T(4,128)S(1)}, ...), branch_computations={%region_57.58_spmd, %region_58.75_spmd} | conditional | flops 2270265856 | bytes 64838092 | solution.py:424
  210.9 51.9 %conditional.131 = (bf16[1,512,96]{1,2,0:T(8,128)(2,1)}, bf16[512,512]{0,1:T(8,128)(2,1)}) conditional(s32[]{:T(128)} %clamp.31, (s32[]{:T(128)}, s32[4,512]{1,0:T(4,128)S(1)}, bf16[4,512,336]{1,2,0:T(8,128)(2,1)}, bf16[96,512]{1,0:T(8,128)(2,1)S(1)}, f32[3,512]{1,0:T(4,128)S(1)}, ...), branch_computations={%region_59.63_spmd, %region_64.66_spmd, %region_67.71_spmd, %regio... | conditional | flops 2270265856 | bytes 63748244
  273.5 8.4 conditional.98
  284.1 28.0 %collective-permute-start.5 = (bf16[512,512]{1,0:T(8,128)(2,1)}, bf16[512,512]{1,0:T(8,128)(2,1)}, u32[]{:S(2)}, u32[]{:S(2)}) collective-permute-start(bf16[512,512]{1,0:T(8,128)(2,1)} %copy.1188), channel_id=1, source_target_pairs={{0,8},{8,16},{16,24},{1,9},{9,17},{17,25},{2,10},{10,18},{18,26},{... | collective-permute-start | bytes 1572872 | tf_op jit(solution)/shard_map/ppermute | solution.py:13
  318.7 11.2 conditional.99
  345.7 23.3 %conditional.101 = (bf16[512,512]{1,0:T(8,128)(2,1)}, f32[512,2048]{1,0:T(8,128)}, f32[2048,512]{1,0:T(8,128)}, f32[512]{0:T(512)}, f32[512]{0:T(512)}, /*index=...) conditional(s32[]{:T(128)} %convert_element_type.2359, ...), branch_computations={%region_120.121_spmd, %region_121.167_spmd} | conditional | flops 6639416320 | bytes 215768416 | solution.py:444
  370.4 34.3 %collective-permute-done.7 = bf16[512,512]{1,0:T(8,128)(2,1)S(1)} collective-permute-done((bf16[512,512]{1,0:T(8,128)(2,1)}, bf16[512,512]{1,0:T(8,128)(2,1)S(1)}, u32[]{:S(2)}, u32[]{:S(2)}) %collective-permute-start.7) | collective-permute-done | bytes 524320 | tf_op jit(solution)/shard_map/ppermute | solution.py:13
  405.5 23.5 %conditional.102 = (bf16[512,512]{1,0:T(8,128)(2,1)}, f32[512,2048]{1,0:T(8,128)}, f32[2048,512]{1,0:T(8,128)}, f32[512]{0:T(512)}, f32[512]{0:T(512)}, /*index=...) conditional(s32[]{:T(128)} %convert_element_type.2360, ...), branch_computations={%region_167.168_spmd, %region_168.217_spmd} | conditional | flops 6639416320 | bytes 224681408 | solution.py:444
  430.3 9.7 collective-permute-done.8
  440.8 23.1 %conditional.103 = (bf16[512,512]{1,0:T(8,128)(2,1)}, f32[512,2048]{1,0:T(8,128)}, f32[2048,512]{1,0:T(8,128)}, f32[512]{0:T(512)}, f32[512]{0:T(512)}, /*index=...) conditional(s32[]{:T(128)} %convert_element_type.2361, ...), branch_computations={%region_217.218_spmd, %region_218.267_spmd} | conditional | flops 6639416320 | bytes 224681408 | solution.py:444
  472.3 126.8 %collective-permute-done.9 = bf16[512,512]{1,0:T(8,128)(2,1)S(1)} collective-permute-done((bf16[512,512]{1,0:T(8,128)(2,1)}, bf16[512,512]{1,0:T(8,128)(2,1)S(1)}, u32[]{:S(2)}, u32[]{:S(2)}) %collective-permute-start.9) | collective-permute-done | bytes 524320 | tf_op jit(solution)/shard_map/ppermute | solution.py:13
  599.9 90.9 %conditional.124 = (bf16[512,512]{1,0:T(8,128)(2,1)}, f32[512,2048]{1,0:T(8,128)}, f32[2048,512]{1,0:T(8,128)}, f32[512]{0:T(512)}, f32[512]{0:T(512)}, /*index=...) conditional(s32[]{:T(128)} %convert_element_type.2362, ...), branch_computations={%region_267.268_spmd, %region_268.317_spmd} | conditional | flops 6639416320 | bytes 224681408 | solution.py:444
  599.9 89.5 %conditional.137 = (f32[512,2048]{1,0:T(8,128)}, f32[2048,512]{1,0:T(8,128)}, f32[512]{0:T(512)}, f32[512]{0:T(512)}, f32[96,512]{1,0:T(8,128)}, /*index=5*/f32[...) conditional(s32[]{:T(128)} %clamp.38, (s32[]{:T(128)}, ...), branch_computations={%region_269.284_spmd, %region_285.293_spmd, %region_294.306_spmd, ... | conditional | flops 6639416320 | bytes 224222208
  698.2 90.7 %conditional.125 = (bf16[512,512]{1,0:T(8,128)(2,1)}, f32[512,2048]{1,0:T(8,128)}, f32[2048,512]{1,0:T(8,128)}, f32[512]{0:T(512)}, f32[512]{0:T(512)}, /*index=...) conditional(s32[]{:T(128)} %convert_element_type.2363, ...), branch_computations={%region_317.318_spmd, %region_318.367_spmd} | conditional | flops 6639416320 | bytes 224681408 | solution.py:444
  698.2 81.2 %conditional.138 = (f32[512,2048]{1,0:T(8,128)}, f32[2048,512]{1,0:T(8,128)}, f32[512]{0:T(512)}, f32[512]{0:T(512)}, f32[96,512]{1,0:T(8,128)}, /*index=5*/f32[...) conditional(s32[]{:T(128)} %clamp.39, (s32[]{:T(128)}, ...), branch_computations={%region_319.334_spmd, %region_335.343_spmd, %region_344.356_spmd, ... | conditional | flops 6639416320 | bytes 224222208
  796.6 90.9 %conditional.126 = (bf16[512,512]{1,0:T(8,128)(2,1)}, f32[512,2048]{1,0:T(8,128)}, f32[2048,512]{1,0:T(8,128)}, f32[512]{0:T(512)}, f32[512]{0:T(512)}, /*index=...) conditional(s32[]{:T(128)} %convert_element_type.2364, ...), branch_computations={%region_367.368_spmd, %region_368.417_spmd} | conditional | flops 6639416320 | bytes 224681408 | solution.py:444
  796.6 81.6 %conditional.139 = (f32[512,2048]{1,0:T(8,128)}, f32[2048,512]{1,0:T(8,128)}, f32[512]{0:T(512)}, f32[512]{0:T(512)}, f32[96,512]{1,0:T(8,128)}, /*index=5*/f32[...) conditional(s32[]{:T(128)} %clamp.40, (s32[]{:T(128)}, ...), branch_computations={%region_369.384_spmd, %region_385.393_spmd, %region_394.406_spmd, ... | conditional | flops 6639416320 | bytes 224222208
  894.8 82.8 %conditional.127 = (f32[512,2048]{1,0:T(8,128)}, f32[2048,512]{1,0:T(8,128)}, f32[512]{0:T(512)}, f32[512]{0:T(512)}, f32[96,512]{1,0:T(8,128)}, /*index=5*/f32[...) conditional(s32[]{:T(128)} %convert_element_type.2365, ...), branch_computations={%region_417.418_spmd, %region_418.467_spmd} | conditional | flops 5878666240 | bytes 224681360 | solution.py:444
  894.8 73.6 %conditional.72 = (f32[512,2048]{1,0:T(8,128)}, f32[2048,512]{1,0:T(8,128)}, f32[512]{0:T(512)}, f32[512]{0:T(512)}, f32[96,512]{1,0:T(8,128)}, /*index=5*/f32[1...) conditional(s32[]{:T(128)} %clamp.41, (s32[]{:T(128)}, ...), branch_computations={%region_419.434_spmd, %region_435.443_spmd, %region_444.456_spmd, ... | conditional | flops 5878666240 | bytes 224222192 | solution.py:403
  989.3 11.8 add_add_fusion
  1013.6 13.6 add_bitcast_fusion
  1029.8 22.3 %all-reduce.58 = (f32[1,512]{1,0:T(1,128)}, f32[1,512]{1,0:T(1,128)}) all-reduce(f32[1,512]{1,0:T(1,128)S(1)} %bitcast.2398, f32[1,512]{1,0:T(1,128)S(1)} %bitcast.2397), channel_id=1, replica_groups=mesh['pipe'=4,'dp'=8] {'dp'}, use_global_device_ids=true, to_apply=%region_474.475 | all-reduce | flops 1024 | bytes 8192 | tf_op jit(solution)/shard_map/psum | solution.py:462
  1056.0 38.2 %all-reduce.56 = (f32[3,512]{1,0:T(4,128)}, f32[2,3,512]{2,0,1:T(2,128)}, f32[2,2048]{1,0:T(2,128)}, f32[2,512]{1,0:T(2,128)}, f32[96]{0:T(128)}) all-reduce(f32[3,512]{1,0:T(4,128)S(1)} %add_add_fusion.7, f32[2,3,512]{2,0,1:T(2,128)S(1)} %add_add_fusion.6, ...), channel_id=1, replica_groups=mesh['pipe'=4,'dp'=8] {'pipe','dp'}, use_global_device_ids=true, to_apply=%region_471.472 | all-reduce | flops 9824 | bytes 78592 | tf_op jit(solution)/shard_map/psum | solution.py:465
  1096.2 79.2 %all-reduce.63.cloned.1.call-done = (f32[96,512]{1,0:T(8,128)}, f32[192,512]{1,0:T(8,128)}, f32[336,512]{1,0:T(8,128)}, f32[512,96]{0,1:T(8,128)}) async-done(((f32[96,512]{1,0:T(8,128)}, f32[192,512]{1,0:T(8,128)}, f32[336,512]{1,0:T(8,128)}, f32[512,96]{0,1:T(8,128)}), (f32[96,512]{1,0:T(8,128)}, f32[192,512]{1,0:T(8,128)}, f32[336,512]{1,0:T(8,128)}, f32[512,96]{0,1:T(8,128)})) %all-reduce.63.cloned.1.call-update) | async-done | bytes 1474576 | tf_op jit(solution)/shard_map/psum | solution.py:465
  1175.3 217.3 %all-reduce.65.cloned.1.call-done = (f32[1,512,2048]{2,1,0:T(8,128)}, f32[1,1024,512]{2,1,0:T(8,128)}) async-done(((f32[1,512,2048]{2,1,0:T(8,128)}, f32[1,1024,512]{2,1,0:T(8,128)}), (f32[1,512,2048]{2,1,0:T(8,128)}, f32[1,1024,512]{2,1,0:T(8,128)})) %all-reduce.65.cloned.1.call-update) | async-done | bytes 6291472 | tf_op jit(solution)/shard_map/psum | solution.py:462
  (692 shorter events, 593.4 us)
Async XLA Ops:
  7.2 24.0 %copy-start.65 = (bf16[96,512]{1,0:T(8,128)(2,1)S(1)}, bf16[96,512]{1,0:T(8,128)(2,1)}, u32[]{:S(2)}) copy-start(bf16[96,512]{1,0:T(8,128)(2,1)} %param.105) | copy-start | bytes 294916
  7.2 24.0 %copy-start.292 = (f32[3,512]{1,0:T(4,128)S(1)}, f32[3,512]{1,0:T(4,128)}, u32[]{:S(2)}) copy-start(f32[3,512]{1,0:T(4,128)} %param.108) | copy-start | bytes 18436
  7.2 24.0 %copy-start.39 = (bf16[192,512]{1,0:T(8,128)(2,1)S(1)}, bf16[192,512]{1,0:T(8,128)(2,1)}, u32[]{:S(2)}) copy-start(bf16[192,512]{1,0:T(8,128)(2,1)} %param.106) | copy-start | bytes 589828
  7.2 24.0 %copy-start.30 = (bf16[336,512]{1,0:T(8,128)(2,1)S(1)}, bf16[336,512]{1,0:T(8,128)(2,1)}, u32[]{:S(2)}) copy-start(bf16[336,512]{1,0:T(8,128)(2,1)} %param.107) | copy-start | bytes 1032196
  7.2 24.0 %copy-start = (bf16[1,512,2048]{2,1,0:T(8,128)(2,1)S(1)}, bf16[1,512,2048]{2,1,0:T(8,128)(2,1)}, u32[]{:S(2)}) copy-start(bf16[1,512,2048]{2,1,0:T(8,128)(2,1)} %param.109) | copy-start | bytes 6291460
  7.2 24.0 %copy-start.282 = (f32[2,3,512]{2,0,1:T(2,128)S(1)}, f32[2,3,512]{2,0,1:T(2,128)}, u32[]{:S(2)}) copy-start(f32[2,3,512]{2,0,1:T(2,128)} %param.113) | copy-start | bytes 36868
  7.2 24.0 %copy-start.75 = (f32[1,512]{1,0:T(1,128)S(1)}, f32[1,512]{1,0:T(1,128)}, u32[]{:S(2)}) copy-start(f32[1,512]{1,0:T(1,128)} %param.111) | copy-start | bytes 6148
  7.3 24.0 %copy-start.283 = (f32[1,512]{1,0:T(1,128)S(1)}, f32[1,512]{1,0:T(1,128)}, u32[]{:S(2)}) copy-start(f32[1,512]{1,0:T(1,128)} %param.112) | copy-start | bytes 6148
  7.3 24.0 %copy-start.217 = (f32[2,2048]{1,0:T(2,128)S(1)}, f32[2,2048]{1,0:T(2,128)}, u32[]{:S(2)}) copy-start(f32[2,2048]{1,0:T(2,128)} %param.114) | copy-start | bytes 49156
  7.3 24.0 %copy-start.293 = (f32[2,512]{1,0:T(2,128)S(1)}, f32[2,512]{1,0:T(2,128)}, u32[]{:S(2)}) copy-start(f32[2,512]{1,0:T(2,128)} %param.115) | copy-start | bytes 12292
  7.3 23.9 %all-gather.2.cloned.1.call-start = ((), (), s32[]{:S(2)}) async-start(), calls=%async_computation.2 | async-start | bytes 1720320 | tf_op jit(solution)/shard_map/all_gather | solution.py:241
  8.1 1086.2 %reduce-scatter.5.cloned.1.call-start = ((), (), s32[]{:S(2)}) async-start(), calls=%async_computation.4 | async-start | bytes 1720320 | tf_op jit(solution)/shard_map/reduce_scatter | solution.py:485
  8.1 5.2 collective-permute-start
  13.3 305.4 %copy-start.343 = (s32[4,512]{1,0:T(4,128)}, s32[4,512]{1,0:T(4,128)S(1)}, u32[]{:S(2)}) copy-start(s32[4,512]{1,0:T(4,128)S(1)} %select_reduce_fusion) | copy-start | bytes 24580
  85.9 3.1 collective-permute-start.1
  145.9 3.1 collective-permute-start.2
  205.6 3.1 collective-permute-start.3
  208.8 58.1 %copy-start.345 = (bf16[1,512,96]{1,2,0:T(8,128)(2,1)S(1)}, bf16[1,512,96]{1,2,0:T(8,128)(2,1)}, u32[]{:S(2)}) copy-start(bf16[1,512,96]{1,2,0:T(8,128)(2,1)} %param.102) | copy-start | bytes 294916
  264.8 8.7 collective-permute-start.4
  281.9 36.8 %copy-start.29 = (bf16[4,512,336]{1,2,0:T(8,128)(2,1)S(1)}, bf16[4,512,336]{1,2,0:T(8,128)(2,1)}, u32[]{:S(2)}) copy-start(bf16[4,512,336]{1,2,0:T(8,128)(2,1)} %all-gather.2.cloned.1.call-done) | copy-start | bytes 4128772
  284.1 34.6 %collective-permute-start.5 = (bf16[512,512]{1,0:T(8,128)(2,1)}, bf16[512,512]{1,0:T(8,128)(2,1)}, u32[]{:S(2)}, u32[]{:S(2)}) collective-permute-start(bf16[512,512]{1,0:T(8,128)(2,1)} %copy.1188), channel_id=1, source_target_pairs={{0,8},{8,16},{16,24},{1,9},{9,17},{17,25},{2,10},{10,18},{18,26},{... | collective-permute-start | bytes 1572872 | tf_op jit(solution)/shard_map/ppermute | solution.py:13
  331.2 11.7 collective-permute-start.6
  369.0 35.6 %collective-permute-start.7 = (bf16[512,512]{1,0:T(8,128)(2,1)}, bf16[512,512]{1,0:T(8,128)(2,1)S(1)}, u32[]{:S(2)}, u32[]{:S(2)}) collective-permute-start(bf16[512,512]{1,0:T(8,128)(2,1)} %get-tuple-element.2724), channel_id=1, source_target_pairs={{8,0},{16,8},{24,16},{9,1},{17,9},{25,17},{10,2},{18,10},{26,18},{... | collective-permute-start | bytes 1572872 | tf_op jit(solution)/shard_map/ppermute | solution.py:13
  429.0 11.0 collective-permute-start.8
  463.9 135.2 %collective-permute-start.9 = (bf16[512,512]{1,0:T(8,128)(2,1)}, bf16[512,512]{1,0:T(8,128)(2,1)S(1)}, u32[]{:S(2)}, u32[]{:S(2)}) collective-permute-start(bf16[512,512]{1,0:T(8,128)(2,1)} %get-tuple-element.2728), channel_id=1, source_target_pairs={{8,0},{16,8},{24,16},{9,1},{17,9},{25,17},{10,2},{18,10},{26,18},{... | collective-permute-start | bytes 1572872 | tf_op jit(solution)/shard_map/ppermute | solution.py:13
  690.8 6.5 collective-permute-start.10
  788.9 6.9 collective-permute-start.11
  887.5 6.5 collective-permute-start.12
  983.4 112.8 %reduce-scatter.3.cloned.1.call-start = ((), (), s32[]{:S(2)}) async-start(), calls=%async_computation.3 | async-start | bytes 491520 | tf_op jit(solution)/shard_map/reduce_scatter | solution.py:482
  989.3 186.1 %all-reduce.63.cloned.1.call-start = ((), (), s32[]{:S(2)}) async-start(), calls=%async_computation.5 | async-start | bytes 2949120 | tf_op jit(solution)/shard_map/psum | solution.py:465
  1001.3 26.0 %collective-permute-start.13 = (bf16[1024,512]{1,0:T(8,128)(2,1)S(1)}, bf16[1024,512]{1,0:T(8,128)(2,1)S(1)}, u32[]{:S(2)}, u32[]{:S(2)}) collective-permute-start(bf16[1024,512]{1,0:T(8,128)(2,1)S(1)} %slice.1975), channel_id=1, source_target_pairs={{8,0},{16,8},{24,16},{9,1},{17,9},{25,17},{10,2},{18,10},{26,18},{... | collective-permute-start | bytes 3145736 | tf_op jit(solution)/shard_map/ppermute | solution.py:13
  1013.6 379.1 %all-reduce.65.cloned.1.call-start = ((), (), s32[]{:S(2)}) async-start(), calls=%async_computation.6 | async-start | bytes 12582912 | tf_op jit(solution)/shard_map/psum | solution.py:462
  (93 other events, 429.4 us)
Sparse Core Ops, SparseCore 0:
  9.7 21.4 all-gather.1
  983.5 27.1 reduce-scatter.4
  1014.0 20.8 reduce-scatter.2
  1042.7 132.6 all-reduce.62
  1180.2 212.4 all-reduce.64
where the time goes:
time: 1420 us; the launch traced here: 1410 us
  waiting for transfers between devices  486 us (34%)
  local copies, waits for them, and re-layouts  236 us (17%)
  loops' own time  209 us (15%)
  matrix products  204 us (14%)
  other arithmetic  141 us (10%)
  blocking collectives  67.1 us (5%)
  starting transfers between devices  54.5 us (4%)
  between operations  15 us (1%)
    psum x1, waiting for transfers between devices, per_device(): lax.psum((totals[0], down_local, totals[2], totals[3]), 'dp')  217 us
    ppermute x14, waiting for transfers between devices, shifted(): return lax.ppermute(array, axis, pairs)  174 us
    unnamed x7, loops' own time  109 us
    another operation x93, local copies, waits for them, and re-layouts  86.4 us
    psum x1, waiting for transfers between devices, per_device(): lax.psum((totals[4], totals[5], totals[6], totals[7], totals[8], totals[9...  79.2 us
    sub x8, matrix products, attention_forward(): weights = jnp.exp(scores - row_max)  60.2 us
    ppermute x14, starting transfers between devices, shifted(): return lax.ppermute(array, axis, pairs)  54.3 us
    another operation x7, loops' own time, per_device(): lax.cond(active_flag, backward_switch, skip_backward, upstream_now, place...  51.6 us
  transfers between devices with their start and end apart: 19, of which 9 were waited for; matrix products, arithmetic and copies ran while one was open for 6% of the time, Pallas kernels for 0%

commit v1 on v0

v1 whole, which is shorter than its diff:
```python
import jax
import jax.numpy as jnp
from jax import lax
from jax.sharding import PartitionSpec as P

HEADS = 8
HEAD_DIM = 64


def shifted(array, axis, by):
    devices = lax.axis_size(axis)
    pairs = [(i, i + by) for i in range(devices) if 0 <= i + by < devices]
    return lax.ppermute(array, axis, pairs)


def as_sent(array):
    return jax.tree.map(lambda a: a.astype(jnp.bfloat16) if a.dtype == jnp.float32 else a, array)


def layer_norm_parts(summed, norm_gain_row, norm_offset):
    centre = summed - jnp.mean(summed, -1, keepdims=True)
    spread = jnp.mean(centre * centre, -1, keepdims=True)
    inverse = lax.rsqrt(spread + 1e-05)
    normed = centre * inverse
    return (normed * norm_gain_row + norm_offset, normed, inverse)


def layer_norm_back(upstream, normed, inverse, norm_gain_row):
    gain_grad = jnp.sum(upstream * normed, 0)
    offset_grad = jnp.sum(upstream, 0)
    scaled = upstream * norm_gain_row
    centred_grad = (
        scaled
        - jnp.mean(scaled, -1, keepdims=True)
        - normed * jnp.mean(scaled * normed, -1, keepdims=True)
    )
    return (centred_grad * inverse, gain_grad, offset_grad)


def row_layout(variate_tallies, lookback_classes, row_len):
    window_end = jnp.cumsum(variate_tallies, -1)
    position = jnp.arange(row_len, dtype=jnp.int32)
    packed_fragment = jnp.sum(
        (position[None, :, None] >= window_end[:, None, :]).astype(jnp.int32), -1
    )
    windows = jnp.arange(variate_tallies.shape[-1], dtype=jnp.int32)
    picked = jnp.sum(
        jnp.where(
            packed_fragment[:, :, None] == windows[None, None, :], lookback_classes[:, None, :], 0
        ),
        -1,
    )
    return (packed_fragment, picked)


def gelu_exact(inputs):
    return jax.nn.gelu(inputs, approximate=False)


def attention_forward(inputs_bf, matrix, biases, norm_gain_row, norm_offset, packed_fragment):
    model_width = inputs_bf.shape[1]
    project = jnp.dot(inputs_bf, matrix[:, : 3 * model_width], preferred_element_type=jnp.float32)
    head_shape = (packed_fragment.shape[0], packed_fragment.shape[1], HEADS, HEAD_DIM)
    query_heads = (project[:, :model_width] + biases[0]).astype(jnp.bfloat16).reshape(head_shape)
    key_heads = project[:, model_width : 2 * model_width].astype(jnp.bfloat16).reshape(head_shape)
    value_heads = (
        (project[:, 2 * model_width :] + biases[1]).astype(jnp.bfloat16).reshape(head_shape)
    )
    scores = jnp.einsum(
        "rqhd,rkhd->rhqk", query_heads, key_heads, preferred_element_type=jnp.float32
    ) * HEAD_DIM ** (-0.5)
    same_window = (packed_fragment[:, :, None] == packed_fragment[:, None, :])[:, None]
    scores = jnp.where(same_window, scores, -1e30)
    row_max = jnp.max(scores, -1, keepdims=True)
    weights = jnp.exp(scores - row_max)
    weights = weights / jnp.sum(weights, -1, keepdims=True)
    weights_bf = weights.astype(jnp.bfloat16)
    mixture = jnp.einsum(
        "rhqk,rkhd->rqhd", weights_bf, value_heads, preferred_element_type=jnp.float32
    )
    mixture_bf = mixture.reshape(-1, model_width).astype(jnp.bfloat16)
    branch = (
        jnp.dot(mixture_bf, matrix[:, 3 * model_width :], preferred_element_type=jnp.float32)
        + biases[2]
    )
    output, normed, inverse = layer_norm_parts(
        inputs_bf.astype(jnp.float32) + branch, norm_gain_row, norm_offset
    )
    return (
        output,
        (query_heads, key_heads, value_heads, weights, weights_bf, mixture_bf, normed, inverse),
    )


def attention_backward(upstream, inputs_bf, matrix, norm_gain_row, saved_parts):
    query_heads, key_heads, value_heads, weights, weights_bf, mixture_bf, normed, inverse = (
        saved_parts
    )
    model_width = inputs_bf.shape[1]
    summed_grad, gain_grad, offset_grad = layer_norm_back(upstream, normed, inverse, norm_gain_row)
    branch_bf = summed_grad.astype(jnp.bfloat16)
    out_matrix_grad = jnp.dot(mixture_bf.T, branch_bf, preferred_element_type=jnp.float32)
    out_bias_grad = jnp.sum(branch_bf.astype(jnp.float32), 0)
    mixture_grad = jnp.dot(
        branch_bf, matrix[:, 3 * model_width :].T, preferred_element_type=jnp.float32
    )
    mixture_grad = mixture_grad.astype(jnp.bfloat16).reshape(query_heads.shape)
    weight_grad = jnp.einsum(
        "rqhd,rkhd->rhqk", mixture_grad, value_heads, preferred_element_type=jnp.float32
    )
    value_grad = jnp.einsum(
        "rhqk,rqhd->rkhd", weights_bf, mixture_grad, preferred_element_type=jnp.float32
    )
    centred = jnp.sum(weights * weight_grad, -1, keepdims=True)
    score_grad = (weights * (weight_grad - centred)).astype(jnp.bfloat16)
    query_grad = jnp.einsum(
        "rhqk,rkhd->rqhd", score_grad, key_heads, preferred_element_type=jnp.float32
    ) * HEAD_DIM ** (-0.5)
    key_grad = jnp.einsum(
        "rhqk,rqhd->rkhd", score_grad, query_heads, preferred_element_type=jnp.float32
    ) * HEAD_DIM ** (-0.5)
    project_grad = jnp.concatenate(
        [
            query_grad.reshape(-1, model_width),
            key_grad.reshape(-1, model_width),
            value_grad.reshape(-1, model_width),
        ],
        1,
    ).astype(jnp.bfloat16)
    in_matrix_grad = jnp.dot(inputs_bf.T, project_grad, preferred_element_type=jnp.float32)
    project_float = project_grad.astype(jnp.float32)
    query_bias_grad = jnp.sum(project_float[:, :model_width], 0)
    value_bias_grad = jnp.sum(project_float[:, 2 * model_width :], 0)
    input_grad = summed_grad + jnp.dot(
        project_grad, matrix[:, : 3 * model_width].T, preferred_element_type=jnp.float32
    )
    matrix_grad = jnp.concatenate([in_matrix_grad, out_matrix_grad], 1)
    bias_grad = jnp.stack([query_bias_grad, value_bias_grad, out_bias_grad])
    return (input_grad, matrix_grad, bias_grad, gain_grad, offset_grad)


def feed_forward(
    inputs_bf, up_matrix, down_matrix, up_offset, down_offset, norm_gain_row, norm_offset
):
    hidden_pre = jnp.dot(inputs_bf, up_matrix, preferred_element_type=jnp.float32) + up_offset
    hidden_bf = gelu_exact(hidden_pre).astype(jnp.bfloat16)
    branch = jnp.dot(hidden_bf, down_matrix, preferred_element_type=jnp.float32) + down_offset
    output, normed, inverse = layer_norm_parts(
        inputs_bf.astype(jnp.float32) + branch, norm_gain_row, norm_offset
    )
    return (output, (hidden_pre, hidden_bf, normed, inverse))


def feed_backward(upstream, inputs_bf, up_matrix, down_matrix, norm_gain_row, saved_parts):
    hidden_pre, hidden_bf, normed, inverse = saved_parts
    summed_grad, gain_grad, offset_grad = layer_norm_back(upstream, normed, inverse, norm_gain_row)
    branch_bf = summed_grad.astype(jnp.bfloat16)
    down_grad = jnp.dot(hidden_bf.T, branch_bf, preferred_element_type=jnp.float32)
    down_offset_grad = jnp.sum(branch_bf.astype(jnp.float32), 0)
    hidden_grad = jnp.dot(branch_bf, down_matrix.T, preferred_element_type=jnp.float32)
    activated, gelu_pull = jax.vjp(gelu_exact, hidden_pre)
    pre_bf = gelu_pull(hidden_grad)[0].astype(jnp.bfloat16)
    up_grad = jnp.dot(inputs_bf.T, pre_bf, preferred_element_type=jnp.float32)
    up_offset_grad = jnp.sum(pre_bf.astype(jnp.float32), 0)
    input_grad = summed_grad + jnp.dot(pre_bf, up_matrix.T, preferred_element_type=jnp.float32)
    return (
        input_grad,
        up_grad,
        down_grad,
        up_offset_grad,
        down_offset_grad,
        gain_grad,
        offset_grad,
    )


def embed_forward(tokens_bf, variate_class, tables, lift_offsets):
    look_width = tokens_bf.shape[1]
    result = jnp.zeros((tokens_bf.shape[0], lift_offsets.shape[1]), jnp.float32)
    for group_index in range(3):
        emb_table = tables[group_index]
        lookback = emb_table.shape[0]
        chosen = (variate_class == group_index).astype(jnp.float32)[:, None]
        result = result + chosen * (
            jnp.dot(
                tokens_bf[:, look_width - lookback :], emb_table, preferred_element_type=jnp.float32
            )
            + lift_offsets[group_index]
        )
    return result


def embed_backward(embed_grad_bf, tokens_bf, variate_class, tables):
    look_width = tokens_bf.shape[1]
    table_grads = []
    bias_grads = []
    series_piece = jnp.zeros(tokens_bf.shape, jnp.float32)
    for group_index in range(3):
        emb_table = tables[group_index]
        lookback = emb_table.shape[0]
        start_col = look_width - lookback
        chosen = (variate_class == group_index).astype(jnp.bfloat16)[:, None]
        masked = embed_grad_bf * chosen
        table_grads.append(
            jnp.dot(tokens_bf[:, start_col:].T, masked, preferred_element_type=jnp.float32)
        )
        bias_grads.append(jnp.sum(masked.astype(jnp.float32), 0))
        spread_back = jnp.dot(masked, emb_table.T, preferred_element_type=jnp.float32)
        series_piece = series_piece + jnp.pad(spread_back, ((0, 0), (start_col, 0)))
    return (table_grads, jnp.stack(bias_grads), series_piece)


def per_device(
    lookback_readings,
    prediction_adjoint,
    variate_tallies,
    lookback_classes,
    brief_lift_table,
    moderate_lift_table,
    distant_lift_table,
    lift_offsets,
    part_entry_arrays,
    part_shrink_lines,
    part_layernorm_scale,
    part_layernorm_offset,
    mixing_offsets,
    expand_offsets,
    shrink_offsets,
    prediction_matrix,
    prediction_offset,
):
    bf16 = jnp.bfloat16
    place = lax.axis_index("pipe")
    sections = lax.axis_size("pipe")
    tokens_bf = lookback_readings[0]
    adjoint = prediction_adjoint[0]
    count = tokens_bf.shape[0]
    rows_mb = variate_tallies.shape[1]
    tallies = lax.dynamic_index_in_dim(variate_tallies, place, 0, False)
    classes = lax.dynamic_index_in_dim(lookback_classes, place, 0, False)
    fragment, picked = row_layout(tallies, classes, count // rows_mb)
    picked = picked.reshape(-1)
    entry, shrink = (
        lax.all_gather(part_entry_arrays, "pipe", axis=0, tiled=True),
        lax.all_gather(part_shrink_lines, "pipe", axis=0, tiled=True),
    )
    scale, offset = (
        lax.all_gather(part_layernorm_scale, "pipe", axis=0, tiled=True),
        lax.all_gather(part_layernorm_offset, "pipe", axis=0, tiled=True),
    )
    tables = (brief_lift_table, moderate_lift_table, distant_lift_table)
    xs = [embed_forward(tokens_bf, picked, tables, lift_offsets).astype(bf16)]
    saved = []
    half = shrink.shape[1]
    for s in range(sections):
        layer = s // 2
        if s % 2 == 0:
            y, kept = attention_forward(
                xs[s], entry[s], mixing_offsets[layer], scale[s], offset[s], fragment
            )
        else:
            down = shrink[2 * layer : 2 * layer + 2].reshape(2 * half, -1)
            y, kept = feed_forward(
                xs[s], entry[s], down, expand_offsets[layer], shrink_offsets[layer], scale[s], offset[s]
            )
        saved.append(kept)
        xs.append(y.astype(bf16))
    last = xs[-1]
    prediction = (
        jnp.dot(last, prediction_matrix, preferred_element_type=jnp.float32) + prediction_offset
    ).astype(bf16)
    proj_w = jnp.dot(last.T, adjoint, preferred_element_type=jnp.float32)
    proj_b = jnp.sum(adjoint.astype(jnp.float32), 0)
    g = jnp.dot(adjoint, prediction_matrix.T, preferred_element_type=jnp.float32)
    entry_grads, down_grads = [None] * sections, [None] * sections
    gains, offsets = [None] * sections, [None] * sections
    att_bias, up_bias, down_bias = [None] * 2, [None] * 2, [None] * 2
    for s in reversed(range(sections)):
        layer = s // 2
        if s % 2 == 0:
            g, entry_grads[s], att_bias[layer], gains[s], offsets[s] = attention_backward(
                g, xs[s], entry[s], scale[s], saved[s]
            )
        else:
            down = shrink[2 * layer : 2 * layer + 2].reshape(2 * half, -1)
            g, entry_grads[s], both, up_bias[layer], down_bias[layer], gains[s], offsets[s] = (
                feed_backward(g, xs[s], entry[s], down, scale[s], saved[s])
            )
            down_grads[2 * layer], down_grads[2 * layer + 1] = both[:half], both[half:]
        g_bf = g.astype(bf16)
        g = g_bf.astype(jnp.float32)
    table_grads, emb_bias, series = embed_backward(g_bf, tokens_bf, picked, tables)
    width = entry.shape[1]
    big = jnp.stack(
        [
            jnp.concatenate(
                [entry_grads[s].astype(bf16).reshape(-1, width), down_grads[s].astype(bf16)], 0
            )
            for s in range(sections)
        ]
    )
    big = lax.psum_scatter(big, "pipe", scatter_dimension=0, tiled=True)[0]
    big = lax.psum(big, "dp").astype(jnp.float32)
    entry_rows = entry.shape[1] * entry.shape[2] // width
    small = lax.psum(
        (
            *table_grads,
            emb_bias,
            jnp.stack(att_bias),
            jnp.stack(up_bias),
            jnp.stack(down_bias),
            proj_w,
            proj_b,
            jnp.stack(gains),
            jnp.stack(offsets),
        ),
        ("pipe", "dp"),
    )
    gain = lax.dynamic_index_in_dim(small[9], place, 0, True)
    bias = lax.dynamic_index_in_dim(small[10], place, 0, True)
    return (
        prediction[None],
        series[None],
        small[0],
        small[1],
        small[2],
        small[3],
        big[:entry_rows].reshape(1, *entry.shape[1:]),
        big[entry_rows:][None],
        gain,
        bias,
        small[4],
        small[5],
        small[6],
        small[7],
        small[8],
    )


def solution(mesh):
    placed = (
        P("pipe", "dp", None),
        P("pipe", "dp", None),
        P(None, "dp", None),
        P(None, "dp", None),
        P(),
        P(),
        P(),
        P(),
        P("pipe", None, None),
        P("pipe", None, None),
        P("pipe", None),
        P("pipe", None),
        P(),
        P(),
        P(),
        P(),
        P(),
    )
    return jax.shard_map(
        per_device,
        mesh=mesh,
        in_specs=placed,
        out_specs=(
            P("pipe", "dp", None),
            P("pipe", "dp", None),
            P(),
            P(),
            P(),
            P(),
            P("pipe", None, None),
            P("pipe", None, None),
            P("pipe", None),
            P("pipe", None),
            P(),
            P(),
            P(),
            P(),
            P(),
        ),
        check_vma=False,
    )
```

time: 1420 us -> 661 us (0.47)
  loops' own time: 209 us -> 0 us
  local copies, waits for them, and re-layouts: 236 us -> 67.9 us
  waiting for transfers between devices: 486 us -> 372 us
  other arithmetic: 141 us -> 27.2 us
  matrix products: 204 us -> 114 us
  starting transfers between devices: 54.5 us -> 0.19 us
    ppermute x14 -> x0, waiting for transfers between devices: 174 us -> none  [shifted(): return lax.ppermute(array, axis, pairs)]
    unnamed x7 -> x0, loops' own time: 109 us -> none
    another operation x15 -> x0, loops' own time: 99.4 us -> none  [the longest x7 51.6 us: per_device(): lax.cond(active_flag, backward_switch, skip_backward, upstream_now, place...]
    reduce_scatter x2 -> x1, waiting for transfers between devices: 0.01 us -> 95.7 us  [per_device(): big = lax.psum_scatter(big, 'pipe', scatter_dimension=0, tiled=True)[0]]
    psum x2, waiting for transfers between devices: 296 us -> 203 us  [the longest x1 127 us: per_device(): lax.psum((*table_grads, emb_bias, jnp.stack(att_bias), jnp.stack(up_bias)...]
    another operation x97 -> x1, local copies, waits for them, and re-layouts: 86.5 us -> 0.66 us  [row_layout(): window_end = jnp.cumsum(variate_tallies, -1)]
    all_gather x1 -> x2, waiting for transfers between devices: 14.9 us -> 72.2 us  [the longest x1 55.4 us: per_device(): lax.all_gather(part_entry_arrays, 'pipe', axis=0, tiled=True)]
    ppermute x14 -> x0, starting transfers between devices: 54.3 us -> none  [shifted(): return lax.ppermute(array, axis, pairs)]
  transfers between devices with their start and end apart: 19 -> 5, of which waited for: 9 -> 5; matrix products, arithmetic and copies ran while one was open for 6% -> 6% of each run, Pallas kernels for 0% -> 0%
where the time goes in v1:
time: 661 us; the launch traced here: 653 us
  waiting for transfers between devices  372 us (56%)
  matrix products  114 us (17%)
  local copies, waits for them, and re-layouts  67.9 us (10%)
  blocking collectives  56 us (8%)
  other arithmetic  27.2 us (4%)
  between operations  15.4 us (2%)
    psum x1, waiting for transfers between devices, per_device(): lax.psum((*table_grads, emb_bias, jnp.stack(att_bias), jnp.stack(up_bias)...  127 us
    reduce_scatter x1, waiting for transfers between devices, per_device(): big = lax.psum_scatter(big, 'pipe', scatter_dimension=0, tiled=True)[0]  95.7 us
    psum x1, waiting for transfers between devices, per_device(): big = lax.psum(big, 'dp').astype(jnp.float32)  76.1 us
    all_gather x1, waiting for transfers between devices, per_device(): lax.all_gather(part_entry_arrays, 'pipe', axis=0, tiled=True)  55.4 us
    psum x1, blocking collectives, per_device(): lax.psum((*table_grads, emb_bias, jnp.stack(att_bias), jnp.stack(up_bias)...  44.5 us
    dot_general x2, matrix products, feed_forward(): jnp.dot(inputs_bf, up_matrix, preferred_element_type=jnp.float32)  24.2 us
    all_gather x1, waiting for transfers between devices, per_device(): lax.all_gather(part_shrink_lines, 'pipe', axis=0, tiled=True)  16.8 us
    unnamed x205, local copies, waits for them, and re-layouts  14.8 us
  transfers between devices with their start and end apart: 5, of which 5 were waited for; matrix products, arithmetic and copies ran while one was open for 6% of the time, Pallas kernels for 0%

profile of v1, /device:TPU:0, one launch (start us, length us, event | category | flops | bytes accessed | tf_op | source)
XLA Modules:
  0.0 653.3 jit_solution(6087958575443937658)
XLA Ops:
  13.3 6.1 all-gather
  19.4 5.4 all-gather.1
  30.2 16.8 %all-gather.7.cloned.1.call-done = bf16[4,1024,512]{2,1,0:T(8,128)(2,1)} async-done(((bf16[1,1024,512]{2,1,0:T(8,128)(2,1)}), bf16[4,1024,512]{2,1,0:T(8,128)(2,1)}) %all-gather.7.cloned.1.call-update) | async-done | bytes 4194320 | tf_op jit(solution)/shard_map/all_gather | solution.py:245
  46.9 4.5 fusion.168
  51.4 55.4 %all-gather.5.cloned.1.call-done = bf16[4,512,2048]{2,1,0:T(8,128)(2,1)} async-done(((bf16[1,512,2048]{2,1,0:T(8,128)(2,1)}), bf16[4,512,2048]{2,1,0:T(8,128)(2,1)}) %all-gather.5.cloned.1.call-update) | async-done | bytes 8388624 | tf_op jit(solution)/shard_map/all_gather | solution.py:244
  106.8 4.1 slice_bitcast_fusion.2
  120.1 7.6 %fusion.177 = (f32[8,512]{1,0:T(8,128)S(1)}, f32[8,512,512]{1,2,0:T(8,128)}) fusion(pred[512,512]{0,1:T(8,128)(4,1)} %broadcast_compare_fusion, bf16[512,8,64]{0,2,1:T(8,128)(2,1)} %bitcast.244, bf16[512,8,64]{0,2,1:T(8,128)(2,1)} %bitcast.246), kind=kOutput, calls=%fused_computation.305 | convolution fusion | flops 276824576 | bytes 9715712 | tf_op jit(solution)/shard_map/sub | solution.py:75
  127.8 4.5 fusion.74
  133.1 14.0 %multiply_convert_fusion.3 = (bf16[512,2048]{1,0:T(8,128)(2,1)S(1)}, f32[512,2048]{1,0:T(8,128)}, f32[512,2048]{1,0:T(8,128)}) fusion(f32[2048]{0:T(1024)S(1)} %bitcast.284, bf16[4,512,2048]{2,1,0:T(8,128)(2,1)} %all-gather.5.cloned.1.call-done, f32[512,512]{0,1:T(8,128)S(1)} %get-tuple-element.154, f32[512]{0:T(512)S(1)} %bitcast.326, ...), kind=kOutput, calls=%fused_computation.35 | convolution fusion | flops 1144258560 | bytes 13647872 | tf_op jit(solution)/shard_map/dot_general | solution.py:145
  156.5 6.5 fusion.180
  163.1 4.5 fusion.80
  169.8 10.2 %multiply_convert_fusion.2 = (bf16[512,2048]{1,0:T(8,128)(2,1)S(1)}, f32[512,2048]{1,0:T(8,128)S(1)}, f32[512,2048]{1,0:T(8,128)S(1)}) fusion(f32[2048]{0:T(1024)S(1)} %bitcast.287, bf16[4,512,2048]{2,1,0:T(8,128)(2,1)S(1)} %bitcast.253, f32[512,512]{0,1:T(8,128)S(1)} %get-tuple-element.161, f32[512]{0:T(512)S(1)} %bitcast.336, f32[512]{0:T(512)S(1)} %bitcast.310, ...), kind=kOutput, calls=%fused_computation.21 | convolution fusion | flops 1144258560 | bytes 13647872 | tf_op jit(solution)/shard_map/dot_general | solution.py:145
  183.3 2.7 convolution_convert_fusion.3
  186.0 2.8 convert_reduce_fusion
  188.8 2.7 convolution_convert_fusion.2
  199.4 2.7 multiply_convert_fusion.1
  209.4 2.7 convolution_convert_fusion.5
  213.8 2.8 convert_reduce_fusion.1
  216.6 2.6 convolution_convert_fusion.4
  219.3 4.2 fusion.107
  237.8 4.3 reshape.521
  248.8 4.5 reshape.520
  254.6 2.6 convert_element_type.306
  257.2 3.2 maximum_bitcast_fusion.2
  262.3 5.6 pad_maximum_fusion
  271.5 95.7 %reduce-scatter.2.cloned.1.call-done = bf16[1,3072,512]{2,1,0:T(8,128)(2,1)} async-done(((bf16[4,3072,512]{2,1,0:T(8,128)(2,1)}), bf16[1,3072,512]{2,1,0:T(8,128)(2,1)}) %reduce-scatter.2.cloned.1.call-update) | async-done | bytes 3145744 | tf_op jit(solution)/shard_map/reduce_scatter | solution.py:302
  367.2 3.4 convert_reduce_fusion.11
  371.8 44.5 %all-reduce.2 = (f32[3,512]{1,0:T(4,128)}, f32[4,512]{1,0:T(4,128)S(1)}, f32[4,512]{1,0:T(4,128)S(1)}, f32[2,3,512]{2,1,0:T(4,128)S(1)}, f32[2,2048]{1,0:T(2,128)}, /*index=5*/f32[2,512]{1,0:T(2,128)}, f32[96]{0:T(128)}) all-reduce(f32[3,512]{1,0:T(4,128)S(1)} %pad_maximum_fusion.7, ...), channel_id=1, replica_groups=mesh['pipe'=4,'dp'=8] {'pipe','dp'}, use_global_device_ids=true, to_apply=%region_31.32 | all-reduce | flops 13920 | bytes 111360 | tf_op jit(solution)/shard_map/psum | solution.py:305
  424.3 76.1 %all-reduce.7.cloned.1.call-done = bf16[3072,512]{1,0:T(8,128)(2,1)} async-done(((bf16[3072,512]{1,0:T(8,128)(2,1)}), bf16[3072,512]{1,0:T(8,128)(2,1)}) %all-reduce.7.cloned.1.call-update) | async-done | bytes 3145744 | tf_op jit(solution)/shard_map/psum | solution.py:303
  500.4 4.1 slice.270
  504.6 5.8 reshape.522
  512.7 126.8 %all-reduce.9.cloned.1.call-done = (f32[96,512]{1,0:T(8,128)}, f32[192,512]{1,0:T(8,128)}, f32[336,512]{1,0:T(8,128)}, f32[512,96]{0,1:T(8,128)}) async-done(((f32[96,512]{1,0:T(8,128)}, f32[192,512]{1,0:T(8,128)}, f32[336,512]{1,0:T(8,128)}, f32[512,96]{0,1:T(8,128)}), (f32[96,512]{1,0:T(8,128)}, f32[192,512]{1,0:T(8,128)}, f32[336,512]{1,0:T(8,128)}, f32[512,96]{0,1:T(8,128)})) %all-reduce.9.cloned.1.call-update) | async-done | bytes 1474576 | tf_op jit(solution)/shard_map/psum | solution.py:305
  (327 shorter events, 98.6 us)
Async XLA Ops:
  7.2 21.7 %copy-start = (bf16[336,512]{1,0:T(8,128)(2,1)S(1)}, bf16[336,512]{1,0:T(8,128)(2,1)}, u32[]{:S(2)}) copy-start(bf16[336,512]{1,0:T(8,128)(2,1)} %param.23) | copy-start | bytes 1032196
  7.2 12.2 %copy-start.74 = (f32[1,512]{1,0:T(1,128)S(1)}, f32[1,512]{1,0:T(1,128)}, u32[]{:S(2)}) copy-start(f32[1,512]{1,0:T(1,128)} %param.28) | copy-start | bytes 6148
  7.2 17.6 %copy-start.71 = (f32[2,512]{1,0:T(2,128)S(1)}, f32[2,512]{1,0:T(2,128)}, u32[]{:S(2)}) copy-start(f32[2,512]{1,0:T(2,128)} %param.31) | copy-start | bytes 12292
  7.2 19.4 %copy-start.69 = (f32[3,512]{1,0:T(4,128)S(1)}, f32[3,512]{1,0:T(4,128)}, u32[]{:S(2)}) copy-start(f32[3,512]{1,0:T(4,128)} %param.24) | copy-start | bytes 18436
  7.2 19.4 %copy-start.56 = (f32[2,3,512]{2,0,1:T(2,128)S(1)}, f32[2,3,512]{2,0,1:T(2,128)}, u32[]{:S(2)}) copy-start(f32[2,3,512]{2,0,1:T(2,128)} %param.29) | copy-start | bytes 36868
  7.2 20.9 %copy-start.10 = (bf16[1,512,336]{1,2,0:T(8,128)(2,1)S(1)}, bf16[1,512,336]{1,2,0:T(8,128)(2,1)}, u32[]{:S(2)}) copy-start(bf16[1,512,336]{1,2,0:T(8,128)(2,1)} %param.17) | copy-start | bytes 1032196
  7.3 20.9 %copy-start.40 = (bf16[192,512]{1,0:T(8,128)(2,1)S(1)}, bf16[192,512]{1,0:T(8,128)(2,1)}, u32[]{:S(2)}) copy-start(bf16[192,512]{1,0:T(8,128)(2,1)} %param.22) | copy-start | bytes 589828
  7.3 21.2 %copy-start.50 = (bf16[96,512]{1,0:T(8,128)(2,1)S(1)}, bf16[96,512]{1,0:T(8,128)(2,1)}, u32[]{:S(2)}) copy-start(bf16[96,512]{1,0:T(8,128)(2,1)} %param.21) | copy-start | bytes 294916
  7.3 39.6 %all-gather.7.cloned.1.call-start = ((), (), s32[]{:S(2)}) async-start(), calls=%async_computation.2 | async-start | bytes 5242880 | tf_op jit(solution)/shard_map/all_gather | solution.py:245
  8.0 98.8 %all-gather.5.cloned.1.call-start = ((), (), s32[]{:S(2)}) async-start(), calls=%async_computation.1 | async-start | bytes 10485760 | tf_op jit(solution)/shard_map/all_gather | solution.py:244
  8.8 358.3 %reduce-scatter.2.cloned.1.call-start = ((), (), s32[]{:S(2)}) async-start(), calls=%async_computation.3 | async-start | bytes 15728640 | tf_op jit(solution)/shard_map/reduce_scatter | solution.py:302
  12.9 17.2 %copy-start.55 = (f32[2,2048]{1,0:T(2,128)S(1)}, f32[2,2048]{1,0:T(2,128)}, u32[]{:S(2)}) copy-start(f32[2,2048]{1,0:T(2,128)} %param.30) | copy-start | bytes 49156
  26.0 121.1 %copy-start.63 = (f32[1,1,512]{2,1,0:T(1,128)}, f32[1,1,512]{2,1,0:T(1,128)S(1)}, u32[]{:S(2)}) copy-start(f32[1,1,512]{2,1,0:T(1,128)S(1)} %get-tuple-element.137) | copy-start | bytes 6148
  110.9 21.4 %copy-start.4 = (bf16[512,2048]{1,0:T(8,128)(2,1)}, bf16[512,2048]{1,0:T(8,128)(2,1)S(1)}, u32[]{:S(2)}) copy-start(bf16[512,2048]{1,0:T(8,128)(2,1)S(1)} %get-tuple-element.114) | copy-start | bytes 6291460
  132.8 14.3 %copy-start.6 = (f32[512,512]{0,1:T(8,128)}, f32[512,512]{0,1:T(8,128)S(1)}, u32[]{:S(2)}) copy-start(f32[512,512]{0,1:T(8,128)S(1)} %get-tuple-element.154) | copy-start | bytes 3145732
  133.1 14.0 %copy-start.30 = (bf16[2,1024,512]{2,1,0:T(8,128)(2,1)S(1)}, bf16[2,1024,512]{2,1,0:T(8,128)(2,1)}, u32[]{:S(2)}) copy-start(bf16[2,1024,512]{2,1,0:T(8,128)(2,1)} %get-tuple-element.116) | copy-start | bytes 6291460
  133.1 14.0 %copy-start.77 = (f32[1,512]{1,0:T(1,128)S(1)}, f32[1,512]{1,0:T(1,128)}, u32[]{:S(2)}) copy-start(f32[1,512]{1,0:T(1,128)} %get-tuple-element.146) | copy-start | bytes 6148
  148.8 18.9 %copy-start.60 = (f32[512]{0:T(512)}, f32[512]{0:T(512)S(1)}, u32[]{:S(2)}) copy-start(f32[512]{0:T(512)S(1)} %add_rsqrt_fusion.2) | copy-start | bytes 6148
  152.8 10.2 %copy-start.24 = (bf16[512,512]{0,1:T(8,128)(2,1)}, bf16[512,512]{0,1:T(8,128)(2,1)S(1)}, u32[]{:S(2)}) copy-start(bf16[512,512]{0,1:T(8,128)(2,1)S(1)} %copy.121) | copy-start | bytes 1572868
  169.7 10.2 %copy-start.76 = (f32[1,512]{1,0:T(1,128)S(1)}, f32[1,512]{1,0:T(1,128)}, u32[]{:S(2)}) copy-start(f32[1,512]{1,0:T(1,128)} %get-tuple-element.145) | copy-start | bytes 6148
  267.9 232.5 %all-reduce.7.cloned.1.call-start = ((), (), s32[]{:S(2)}) async-start(), calls=%async_computation.4 | async-start | bytes 6291456 | tf_op jit(solution)/shard_map/psum | solution.py:303
  269.4 97.8 %copy-start.5 = (bf16[512,2048]{1,0:T(8,128)(2,1)S(1)}, bf16[512,2048]{1,0:T(8,128)(2,1)}, u32[]{:S(2)}) copy-start(bf16[512,2048]{1,0:T(8,128)(2,1)} %copy-done.4) | copy-start | bytes 6291460
  269.4 97.8 %copy-start.57 = (bf16[512]{0:T(512)(128)(2,1)S(1)}, bf16[512]{0:T(512)(128)(2,1)}, u32[]{:S(2)}) copy-start(bf16[512]{0:T(512)(128)(2,1)} %get-tuple-element.147) | copy-start | bytes 3076
  269.4 97.8 %copy-start.58 = (bf16[512]{0:T(512)(128)(2,1)S(1)}, bf16[512]{0:T(512)(128)(2,1)}, u32[]{:S(2)}) copy-start(bf16[512]{0:T(512)(128)(2,1)} %get-tuple-element.103) | copy-start | bytes 3076
  367.1 272.4 %all-reduce.9.cloned.1.call-start = ((), (), s32[]{:S(2)}) async-start(), calls=%async_computation.5 | async-start | bytes 2949120 | tf_op jit(solution)/shard_map/psum | solution.py:305
  370.8 46.7 %copy-start.52 = (bf16[512,96]{0,1:T(8,128)(2,1)S(1)}, bf16[512,96]{0,1:T(8,128)(2,1)}, u32[]{:S(2)}) copy-start(bf16[512,96]{0,1:T(8,128)(2,1)} %param.32) | copy-start | bytes 294916
  370.8 46.7 %copy-start.89 = (f32[96]{0:T(128)S(1)}, f32[96]{0:T(128)}, u32[]{:S(2)}) copy-start(f32[96]{0:T(128)} %param.33) | copy-start | bytes 1156
  370.8 47.5 %copy-start.39 = (bf16[1,512,96]{1,2,0:T(8,128)(2,1)S(1)}, bf16[1,512,96]{1,2,0:T(8,128)(2,1)}, u32[]{:S(2)}) copy-start(bf16[1,512,96]{1,2,0:T(8,128)(2,1)} %param.18) | copy-start | bytes 294916
  370.9 48.5 %copy-start.11 = (bf16[1,512,336]{1,2,0:T(8,128)(2,1)S(1)}, bf16[1,512,336]{1,2,0:T(8,128)(2,1)}, u32[]{:S(2)}) copy-start(bf16[1,512,336]{1,2,0:T(8,128)(2,1)} %param.17) | copy-start | bytes 1032196
  370.9 48.5 %copy-start.70 = (bf16[512]{0:T(512)(128)(2,1)S(1)}, bf16[512]{0:T(512)(128)(2,1)}, u32[]{:S(2)}) copy-start(bf16[512]{0:T(512)(128)(2,1)} %get-tuple-element.149) | copy-start | bytes 3076
  370.9 50.5 %copy-start.41 = (bf16[192,512]{1,0:T(8,128)(2,1)S(1)}, bf16[192,512]{1,0:T(8,128)(2,1)}, u32[]{:S(2)}) copy-start(bf16[192,512]{1,0:T(8,128)(2,1)} %param.22) | copy-start | bytes 589828
  371.6 51.3 %copy-start.51 = (bf16[96,512]{1,0:T(8,128)(2,1)S(1)}, bf16[96,512]{1,0:T(8,128)(2,1)}, u32[]{:S(2)}) copy-start(bf16[96,512]{1,0:T(8,128)(2,1)} %param.21) | copy-start | bytes 294916
  (73 other events, 268.1 us)
Sparse Core Ops, SparseCore 0:
  9.7 37.2 all-gather.6
  48.5 58.2 all-gather.4
  268.0 99.0 reduce-scatter.1
  370.5 129.8 all-reduce.6
  508.3 131.2 all-reduce.8

commit v2 on v1

v2 whole, which is shorter than its diff:
```python
import functools

import jax
import jax.numpy as jnp
from jax import lax
from jax.experimental import pallas as pl
from jax.experimental.pallas import tpu as pltpu
from jax.sharding import PartitionSpec as P

HEADS = 8
HEAD_DIM = 64
F32 = jnp.float32
BF16 = jnp.bfloat16
SHARED_ROWS = 768
VECTOR_ROW = 720


def nn(a, b):
    return lax.dot_general(a, b, (((1,), (0,)), ((), ())), preferred_element_type=F32)


def nt(a, b):
    return lax.dot_general(a, b, (((1,), (1,)), ((), ())), preferred_element_type=F32)


def tn(a, b):
    return lax.dot_general(a, b, (((0,), (0,)), ((), ())), preferred_element_type=F32)


def normalise(z):
    centre = z - jnp.mean(z, -1, keepdims=True)
    inverse = lax.rsqrt(jnp.mean(centre * centre, -1, keepdims=True) + 1e-05)
    return centre * inverse, inverse


def norm_back(upstream, z, gain):
    normed, inverse = normalise(z)
    gain_grad = jnp.sum(upstream * normed, 0, keepdims=True)
    offset_grad = jnp.sum(upstream, 0, keepdims=True)
    scaled = upstream * gain
    back = inverse * (
        scaled
        - jnp.mean(scaled, -1, keepdims=True)
        - normed * jnp.mean(scaled * normed, -1, keepdims=True)
    )
    return back, gain_grad, offset_grad


def gelu_both(u):
    bell = jnp.exp(u * u * -0.5)
    t = 1.0 / (1.0 + (0.3275911 * 0.5**0.5) * jnp.abs(u))
    poly = t * (
        0.127414796
        + t * (-0.142248368 + t * (0.7107068705 + t * (-0.7265760135 + t * 0.5307027145)))
    )
    half = poly * bell
    phi = jnp.where(u >= 0, 1.0 - half, half)
    return u * phi, phi + u * bell * 0.3989422804014327


def same_window_bias(seg_col, seg_row):
    return jnp.where(seg_col == seg_row, 0.0, -1e30).astype(F32)


class Choice:
    def __init__(self, index, sources, place, sem):
        self.index = index
        self.copies = [pltpu.make_async_copy(s, place, sem) for s in sources]

    def start(self):
        for k, copy in enumerate(self.copies):
            pl.when(self.index == k)(copy.start)

    def wait(self):
        for k, copy in enumerate(self.copies):
            pl.when(self.index == k)(copy.wait)


def attention_forward_kernel(
    at_ref, w0, w1, w2, w3, x_ref, bias_ref, norm_ref, segc_ref, segr_ref,
    y_ref, z_ref, qkv_ref, o_ref, lse_ref, mask_ref, w_ref, sem,
):
    choice = Choice(at_ref[0], (w0, w1, w2, w3), w_ref, sem.at[0])
    choice.start()
    width = x_ref.shape[1]
    x = x_ref[...]
    mask_ref[...] = same_window_bias(segc_ref[...], segr_ref[...])
    choice.wait()
    qkv_ref[:, :width] = ((nn(x, w_ref[:, :width]) + bias_ref[0:1, :]) * HEAD_DIM**-0.5).astype(BF16)
    qkv_ref[:, width : 2 * width] = nn(x, w_ref[:, width : 2 * width]).astype(BF16)
    qkv_ref[:, 2 * width : 3 * width] = (
        nn(x, w_ref[:, 2 * width : 3 * width]) + bias_ref[1:2, :]
    ).astype(BF16)
    pair = 2 * HEAD_DIM
    low = lax.broadcasted_iota(jnp.int32, (1, pair), 1) < HEAD_DIM
    for p in range(HEADS // 2):
        q2 = qkv_ref[:, p * pair : (p + 1) * pair]
        k2 = qkv_ref[:, width + p * pair : width + (p + 1) * pair]
        v2 = qkv_ref[:, 2 * width + p * pair : 2 * width + (p + 1) * pair]
        v2t = v2.T
        parts = []
        for h in range(2):
            kh = jnp.where(low if h == 0 else ~low, k2, jnp.zeros_like(k2))
            s = nt(kh, q2) + mask_ref[...]
            top = jnp.max(s, 0, keepdims=True)
            e = jnp.exp(s - top)
            total = jnp.sum(e, 0, keepdims=True)
            lse_ref[2 * p + h : 2 * p + h + 1, :] = top + jnp.log(total)
            ot = nn(v2t[h * HEAD_DIM : (h + 1) * HEAD_DIM, :], e.astype(BF16))
            parts.append(ot * (1.0 / total))
        o_ref[:, p * pair : (p + 1) * pair] = jnp.concatenate(parts, 0).T.astype(BF16)
    z = x.astype(F32) + (nn(o_ref[...], w_ref[:, 3 * width :]) + bias_ref[2:3, :])
    z_ref[...] = z
    y_ref[...] = (normalise(z)[0] * norm_ref[0:1, :] + norm_ref[1:2, :]).astype(BF16)


def feed_core(x, up_ref, down_ref, upb_ref, h_ref, d_ref, block=512):
    total = None
    for c in range(0, up_ref.shape[1], block):
        u = nn(x, up_ref[:, c : c + block]) + upb_ref[:, c : c + block]
        h, d = gelu_both(u)
        hb = h.astype(BF16)
        h_ref[:, c : c + block] = hb
        d_ref[:, c : c + block] = d.astype(BF16)
        part = nn(hb, down_ref[c : c + block, :])
        total = part if total is None else total + part
    return total


def feed_weights(at_ref, ups, downs, up_ref, down_ref, sem):
    half = down_ref.shape[0] // 2
    loads = [Choice(at_ref[0], ups, up_ref, sem.at[0])]
    loads += [
        Choice(at_ref[1 + h], downs, down_ref.at[pl.ds(h * half, half)], sem.at[1 + h]) for h in range(2)
    ]
    for one in loads:
        one.start()
    return loads


def feed_forward_kernel(
    at_ref, u0, u1, u2, u3, d0, d1, d2, d3, x_ref, upb_ref, downb_ref, norm_ref,
    y_ref, z_ref, h_ref, d_ref, up_ref, down_ref, sem,
):
    loads = feed_weights(at_ref, (u0, u1, u2, u3), (d0, d1, d2, d3), up_ref, down_ref, sem)
    x = x_ref[...]
    for one in loads:
        one.wait()
    f = feed_core(x, up_ref, down_ref, upb_ref, h_ref, d_ref)
    z = x.astype(F32) + (f + downb_ref[...])
    z_ref[...] = z
    y_ref[...] = (normalise(z)[0] * norm_ref[0:1, :] + norm_ref[1:2, :]).astype(BF16)


def feed_back_core(
    core, upstream, x, z, h_ref, d_ref, up_ref, down_ref, gain,
    keep_ref, send_ref, upb_ref, xt_ref, gx_acc,
):
    back, gain_grad, offset_grad = norm_back(upstream, z, gain)
    back_bf = back.astype(BF16)
    downb = jnp.sum(back_bf.astype(F32), 0, keepdims=True)
    gx_acc[...] = back
    xt_ref[...] = x.T
    width = x.shape[1]
    rows = width // 2
    blocks = up_ref.shape[1] // width
    for j in range(blocks):
        b = lax.rem(j + core * (blocks // 2), blocks)
        cols = pl.ds(pl.multiple_of(b * width, width), width)
        gu = (nt(back_bf, down_ref[cols, :]) * d_ref[:, cols].astype(F32)).astype(BF16)
        down_out = keep_ref if j < blocks // 2 else send_ref
        at = blocks * rows + (j % (blocks // 2)) * width
        down_out[at : at + width, :] = tn(h_ref[:, cols], back_bf).astype(BF16)
        mine = pl.ds(pl.multiple_of(core * rows, rows), rows)
        other = pl.ds(pl.multiple_of((1 - core) * rows, rows), rows)
        at = pl.ds(pl.multiple_of(b * rows, rows), rows)
        keep_ref[at, :] = nn(xt_ref[mine, :], gu).astype(BF16)
        send_ref[at, :] = nn(xt_ref[other, :], gu).astype(BF16)
        upb_ref[pl.ds(b, 1), :] = jnp.sum(gu.astype(F32), 0, keepdims=True)
        gx_acc[...] += nt(gu, up_ref[:, cols])
    return gain_grad, offset_grad, downb


def feed_back_kernel(
    at_ref, u0, u1, u2, u3, d0, d1, d2, d3, g_ref, x_ref, z_ref, h_ref, d_ref, norm_ref,
    gx_ref, keep_ref, send_ref, upb_ref, vec_ref, up_ref, down_ref, xt_ref, gx_acc, sem,
):
    loads = feed_weights(at_ref, (u0, u1, u2, u3), (d0, d1, d2, d3), up_ref, down_ref, sem)
    for one in loads:
        one.wait()
    gain_grad, offset_grad, downb = feed_back_core(
        at_ref[3], g_ref[...].astype(F32), x_ref[...], z_ref[...], h_ref, d_ref, up_ref, down_ref,
        norm_ref[0:1, :], keep_ref, send_ref, upb_ref, xt_ref, gx_acc,
    )
    gx_ref[...] = gx_acc[...].astype(BF16)
    vec_ref[...] = jnp.concatenate([gain_grad, offset_grad, downb], 0)


def last_feed_kernel(
    at_ref, u0, u1, u2, u3, d0, d1, d2, d3,
    x_ref, upb_ref, downb_ref, norm_ref, pm_ref, pb_ref, adj_ref,
    pred_ref, gpm_ref, gpb_ref, gx_ref, keep_ref, send_ref, gupb_ref, vec_ref,
    h_ref, d_ref, up_ref, down_ref, xt_ref, gx_acc, sem,
):
    loads = feed_weights(at_ref, (u0, u1, u2, u3), (d0, d1, d2, d3), up_ref, down_ref, sem)
    x = x_ref[...]
    for one in loads:
        one.wait()
    f = feed_core(x, up_ref, down_ref, upb_ref, h_ref, d_ref)
    z = x.astype(F32) + (f + downb_ref[...])
    y = (normalise(z)[0] * norm_ref[0:1, :] + norm_ref[1:2, :]).astype(BF16)
    pm = pm_ref[...]
    adj = adj_ref[...]
    pred_ref[...] = (nn(y, pm) + pb_ref[...]).astype(BF16)
    gpm_ref[...] = tn(adj, y)
    gpb_ref[...] = jnp.sum(adj.astype(F32), 0, keepdims=True)
    gain_grad, offset_grad, downb = feed_back_core(
        at_ref[3], nt(adj, pm), x, z, h_ref, d_ref, up_ref, down_ref,
        norm_ref[0:1, :], keep_ref, send_ref, gupb_ref, xt_ref, gx_acc,
    )
    gx_ref[...] = gx_acc[...].astype(BF16)
    vec_ref[...] = jnp.concatenate([gain_grad, offset_grad, downb], 0)


def attention_back_kernel(
    at_ref, w0, w1, w2, w3, g_ref, x_ref, z_ref, qkv_ref, o_ref, lse_ref, norm_ref, segc_ref, segr_ref,
    gx_ref, keep_ref, send_ref, vec_ref, mask_ref, gqkv_ref, go_ref, w_ref, xt_ref, sem,
):
    choice = Choice(at_ref[0], (w0, w1, w2, w3), w_ref, sem.at[0])
    choice.start()
    core = at_ref[1]
    width = x_ref.shape[1]
    rows = width // 2
    mine = pl.ds(pl.multiple_of(core * rows, rows), rows)
    other = pl.ds(pl.multiple_of((1 - core) * rows, rows), rows)
    back, gain_grad, offset_grad = norm_back(g_ref[...].astype(F32), z_ref[...], norm_ref[0:1, :])
    ga = back.astype(BF16)
    gab = jnp.sum(ga.astype(F32), 0, keepdims=True)
    xt_ref[...] = o_ref[...].T
    keep_ref[3 * rows : 4 * rows, :] = nn(xt_ref[mine, :], ga).astype(BF16)
    send_ref[3 * rows : 4 * rows, :] = nn(xt_ref[other, :], ga).astype(BF16)
    mask_ref[...] = same_window_bias(segc_ref[...], segr_ref[...])
    choice.wait()
    go_ref[...] = nt(ga, w_ref[:, 3 * width :]).astype(BF16)
    pair = 2 * HEAD_DIM
    low = lax.broadcasted_iota(jnp.int32, (1, pair), 1) < HEAD_DIM
    for p in range(HEADS // 2):
        q2 = qkv_ref[:, p * pair : (p + 1) * pair]
        k2 = qkv_ref[:, width + p * pair : width + (p + 1) * pair]
        v2 = qkv_ref[:, 2 * width + p * pair : 2 * width + (p + 1) * pair]
        go2 = go_ref[:, p * pair : (p + 1) * pair]
        o2 = o_ref[:, p * pair : (p + 1) * pair]
        k2t = k2.T
        prod = (go2.astype(F32) * o2.astype(F32)).T
        gq, gk, gv = [], None, None
        for h in range(2):
            own = low if h == 0 else ~low
            zero = jnp.zeros_like(k2)
            lanes = slice(h * HEAD_DIM, (h + 1) * HEAD_DIM)
            centred = jnp.sum(prod[lanes, :], 0, keepdims=True)
            s = nt(jnp.where(own, k2, zero), q2) + mask_ref[...]
            weights = jnp.exp(s - lse_ref[2 * p + h : 2 * p + h + 1, :])
            gp = nt(jnp.where(own, v2, zero), go2)
            gs = (weights * (gp - centred)).astype(BF16)
            gv_part = nn(weights.astype(BF16), jnp.where(own, go2, zero))
            gk_part = nn(gs, jnp.where(own, q2, zero))
            gv = gv_part if gv is None else gv + gv_part
            gk = gk_part if gk is None else gk + gk_part
            gq.append(nn(k2t[lanes, :], gs) * HEAD_DIM**-0.5)
        cols = slice(p * pair, (p + 1) * pair)
        gqkv_ref[:, cols] = jnp.concatenate(gq, 0).T.astype(BF16)
        gqkv_ref[:, width + p * pair : width + (p + 1) * pair] = gk.astype(BF16)
        gqkv_ref[:, 2 * width + p * pair : 2 * width + (p + 1) * pair] = gv.astype(BF16)
    xt_ref[...] = x_ref[...].T
    for b in range(3):
        part = gqkv_ref[:, b * width : (b + 1) * width]
        keep_ref[b * rows : (b + 1) * rows, :] = nn(xt_ref[mine, :], part).astype(BF16)
        send_ref[b * rows : (b + 1) * rows, :] = nn(xt_ref[other, :], part).astype(BF16)
    gqkv = gqkv_ref[...]
    gqb = jnp.sum(gqkv[:, :width].astype(F32), 0, keepdims=True)
    gvb = jnp.sum(gqkv[:, 2 * width :].astype(F32), 0, keepdims=True)
    gx_ref[...] = (back + nt(gqkv, w_ref[:, : 3 * width])).astype(BF16)
    vec_ref[...] = jnp.concatenate([gain_grad, offset_grad, gqb, gvb, gab], 0)


def padded_table(t_ref, look):
    table = t_ref[...]
    skip = look - table.shape[0]
    if skip:
        table = jnp.concatenate([jnp.zeros((skip, table.shape[1]), BF16), table], 0)
    return table, skip


def embed_kernel(tok_ref, cls_ref, t0_ref, t1_ref, t2_ref, off_ref, x_ref):
    tok = tok_ref[...]
    cls = cls_ref[...]
    total = None
    for g, t_ref in enumerate((t0_ref, t1_ref, t2_ref)):
        chosen = cls == g
        masked = jnp.where(chosen, tok, jnp.zeros_like(tok))
        table, _ = padded_table(t_ref, tok.shape[1])
        part = nn(masked, table) + jnp.where(chosen, off_ref[g : g + 1, :], 0.0)
        total = part if total is None else total + part
    x_ref[...] = total.astype(BF16)


def embed_back_kernel(
    core_ref, g_ref, tok_ref, cls_ref, t0_ref, t1_ref, t2_ref,
    gpm_ref, gpb_ref, vec0_ref, vec1_ref, vec2_ref, vec3_ref, upb0_ref, upb1_ref,
    series_ref, keep_ref, send_ref, all_ref,
):
    tok = tok_ref[...]
    cls = cls_ref[...]
    g = g_ref[...]
    tokt = tok.T
    series = None
    sums = []
    at = 0
    for i, t_ref in enumerate((t0_ref, t1_ref, t2_ref)):
        masked = jnp.where(cls == i, g, jnp.zeros_like(g))
        table, skip = padded_table(t_ref, tok.shape[1])
        part = nt(masked, table)
        series = part if series is None else series + part
        count = table.shape[0] - skip
        all_ref[at : at + count, :] = nn(tokt, masked)[skip:, :].astype(BF16)
        at += count
        sums.append(jnp.sum(masked.astype(F32), 0, keepdims=True))
    series_ref[...] = series
    all_ref[at : at + gpm_ref.shape[0], :] = gpm_ref[...].astype(BF16)
    width = g.shape[1]
    gpb = jnp.concatenate(
        [gpb_ref[...], jnp.zeros((1, width - gpb_ref.shape[1]), F32)], 1
    )
    rows = [gpb, *sums, vec0_ref[2:5, :], vec2_ref[2:5, :], upb0_ref[...], upb1_ref[...]]
    rows += [vec1_ref[2:3, :], vec3_ref[2:3, :]]
    vecs = (vec0_ref, vec1_ref, vec2_ref, vec3_ref)
    rows += [v[0:1, :] for v in vecs] + [v[1:2, :] for v in vecs]
    used = sum(r.shape[0] for r in rows)
    rows.append(jnp.zeros((SHARED_ROWS - VECTOR_ROW - used, width), F32))
    all_ref[VECTOR_ROW:SHARED_ROWS, :] = jnp.concatenate(rows, 0).astype(BF16)
    if all_ref.shape[0] > SHARED_ROWS:
        all_ref[SHARED_ROWS:, :] = jnp.zeros((all_ref.shape[0] - SHARED_ROWS, width), BF16)
    half = all_ref.shape[0] // 2
    core = core_ref[0]
    keep_ref[...] = all_ref[pl.ds(pl.multiple_of(core * half, half), half), :]
    send_ref[...] = all_ref[pl.ds(pl.multiple_of((1 - core) * half, half), half), :]


def shared_out_kernel(
    at_ref, mine_ref, other_ref,
    t0_ref, t1_ref, t2_ref, embb_ref, gain_ref, offset_ref, att_ref, up_ref, down_ref, pw_ref, pb_ref,
    all_ref,
):
    half = all_ref.shape[0] // 2
    core = at_ref[0]
    place = at_ref[1]
    all_ref[pl.ds(pl.multiple_of(core * half, half), half), :] = mine_ref[...].astype(F32)
    all_ref[pl.ds(pl.multiple_of((1 - core) * half, half), half), :] = other_ref[...].astype(F32)
    at = 0
    for out in (t0_ref, t1_ref, t2_ref):
        out[...] = all_ref[at : at + out.shape[0], :]
        at += out.shape[0]
    pw_ref[...] = all_ref[at : at + pw_ref.shape[1], :].T
    v = VECTOR_ROW
    width = all_ref.shape[1]
    pb_ref[...] = all_ref[v : v + 1, : pb_ref.shape[1]]
    embb_ref[...] = all_ref[v + 1 : v + 4, :]
    att_ref[0, :, :] = all_ref[v + 4 : v + 7, :]
    att_ref[1, :, :] = all_ref[v + 7 : v + 10, :]
    for l in range(2):
        for b in range(4):
            row = v + 10 + 4 * l + b
            up_ref[l : l + 1, b * width : (b + 1) * width] = all_ref[row : row + 1, :]
    down_ref[...] = all_ref[v + 18 : v + 20, :]
    gain_ref[...] = all_ref[pl.ds(v + 20 + place, 1), :]
    offset_ref[...] = all_ref[pl.ds(v + 24 + place, 1), :]


def entry_out_kernel(core_ref, att_ref, att_other_ref, up_ref, up_other_ref, out_ref):
    rows = out_ref.shape[0] // 2
    width = att_ref.shape[1]

    def write(low, high):
        for b in range(out_ref.shape[1] // width):
            cols = slice(b * width, (b + 1) * width)
            out_ref[:rows, cols] = low[b * rows : (b + 1) * rows, :].astype(F32)
            out_ref[rows:, cols] = high[b * rows : (b + 1) * rows, :].astype(F32)

    pl.when(core_ref[0] == 0)(lambda: write(att_ref, att_other_ref))
    pl.when(core_ref[0] == 1)(lambda: write(up_other_ref, up_ref))


def call(kernel, kinds, outs, scratch=(), vmem=32 << 20, flops=0, nbytes=0):
    spaces = {
        "s": pl.BlockSpec(memory_space=pltpu.SMEM),
        "a": pl.BlockSpec(memory_space=pl.ANY),
        "v": pl.BlockSpec(memory_space=pltpu.VMEM),
    }

    def run(*args):
        return pl.pallas_call(
            kernel,
            out_shape=[jax.ShapeDtypeStruct(s, d) for s, d in outs],
            in_specs=[spaces[k] for k in kinds],
            out_specs=[spaces["v"]] * len(outs),
            scratch_shapes=list(scratch),
            compiler_params=pltpu.CompilerParams(vmem_limit_bytes=vmem),
            cost_estimate=pl.CostEstimate(flops=flops, bytes_accessed=nbytes, transcendentals=0),
        )(*args)

    return run


def scalars(*values):
    return jnp.stack([jnp.asarray(v, jnp.int32) for v in values])


def attention_fwd(at, weights, x, bias, norm, segc, segr):
    n, d = x.shape
    return call(
        attention_forward_kernel,
        "saaaavvvvv",
        [((n, d), BF16), ((n, d), F32), ((n, 3 * d), BF16), ((n, d), BF16), ((HEADS, n), F32)],
        [pltpu.VMEM((n, n), F32), pltpu.VMEM(weights[0].shape, BF16), pltpu.SemaphoreType.DMA((1,))],
        flops=5_000_000_000,
    )(at, *weights, x, bias, norm, segc, segr)


def feed_scratch(up, down):
    return [
        pltpu.VMEM(up.shape, BF16),
        pltpu.VMEM((2 * down.shape[0], down.shape[1]), BF16),
    ]


def feed_fwd(at, ups, downs, x, upb, downb, norm):
    n, d = x.shape
    ff = ups[0].shape[1]
    return call(
        feed_forward_kernel,
        "saaaaaaaavvvv",
        [((n, d), BF16), ((n, d), F32), ((n, ff), BF16), ((n, ff), BF16)],
        feed_scratch(ups[0], downs[0]) + [pltpu.SemaphoreType.DMA((3,))],
        flops=5_000_000_000,
    )(at, *ups, *downs, x, upb, downb, norm)


def last_feed(at, ups, downs, x, upb, downb, norm, pm, pb, adj):
    n, d = x.shape
    ff = ups[0].shape[1]
    out = pm.shape[1]
    share = ff // d * (d // 2) + ff // 2
    return call(
        last_feed_kernel,
        "saaaaaaaavvvvvvv",
        [
            ((n, out), BF16), ((out, d), F32), ((1, out), F32), ((n, d), BF16),
            ((share, d), BF16), ((share, d), BF16), ((ff // d, d), F32), ((3, d), F32),
        ],
        [pltpu.VMEM((n, ff), BF16), pltpu.VMEM((n, ff), BF16)]
        + feed_scratch(ups[0], downs[0])
        + [pltpu.VMEM((d, n), BF16), pltpu.VMEM((n, d), F32), pltpu.SemaphoreType.DMA((3,))],
        flops=8_000_000_000,
    )(at, *ups, *downs, x, upb, downb, norm, pm, pb, adj)


def feed_bwd(at, ups, downs, g, x, z, h, dd, norm):
    n, d = x.shape
    ff = ups[0].shape[1]
    share = ff // d * (d // 2) + ff // 2
    return call(
        feed_back_kernel,
        "saaaaaaaavvvvvv",
        [((n, d), BF16), ((share, d), BF16), ((share, d), BF16), ((ff // d, d), F32), ((3, d), F32)],
        feed_scratch(ups[0], downs[0])
        + [pltpu.VMEM((d, n), BF16), pltpu.VMEM((n, d), F32), pltpu.SemaphoreType.DMA((3,))],
        flops=6_000_000_000,
    )(at, *ups, *downs, g, x, z, h, dd, norm)


def attention_bwd(at, weights, g, x, z, qkv, o, lse, norm, segc, segr):
    n, d = x.shape
    return call(
        attention_back_kernel,
        "saaaavvvvvvvvv",
        [((n, d), BF16), ((2 * d, d), BF16), ((2 * d, d), BF16), ((5, d), F32)],
        [
            pltpu.VMEM((n, n), F32), pltpu.VMEM((n, 3 * d), BF16), pltpu.VMEM((n, d), BF16),
            pltpu.VMEM(weights[0].shape, BF16), pltpu.VMEM((d, n), BF16), pltpu.SemaphoreType.DMA((1,)),
        ],
        flops=7_000_000_000,
    )(at, *weights, g, x, z, qkv, o, lse, norm, segc, segr)


def embed_fwd(tok, cls, t0, t1, t2, off):
    return call(embed_kernel, "vvvvvv", [((tok.shape[0], t0.shape[1]), BF16)], flops=1_500_000_000)(
        tok, cls, t0, t1, t2, off
    )[0]


def embed_bwd(core, g, tok, cls, tables, small, rows):
    d = g.shape[1]
    return call(
        embed_back_kernel,
        "svvvvvv" + "v" * len(small),
        [(tok.shape, F32), ((rows // 2, d), BF16), ((rows // 2, d), BF16)],
        [pltpu.VMEM((rows, d), BF16)],
        flops=2_000_000_000,
    )(core, g, tok, cls, *tables, *small)


def shared_out(at, mine, other, tables, horizon, ff):
    d = mine.shape[1]
    return call(
        shared_out_kernel,
        "svv",
        [(t.shape, F32) for t in tables]
        + [((3, d), F32), ((1, d), F32), ((1, d), F32), ((2, 3, d), F32), ((2, ff), F32), ((2, d), F32)]
        + [((d, horizon), F32), ((1, horizon), F32)],
        [pltpu.VMEM((2 * mine.shape[0], d), F32)],
        nbytes=4_000_000,
    )(at, mine, other)


def entry_out(core, att, att_other, up, up_other, shape):
    return call(entry_out_kernel, "svvvv", [(shape, F32)], nbytes=8_000_000)(
        core, att, att_other, up, up_other
    )[0]


def row_layout(variate_tallies, lookback_classes, row_len):
    window_end = jnp.cumsum(variate_tallies, -1)
    position = jnp.arange(row_len, dtype=jnp.int32)
    packed_fragment = jnp.sum(
        (position[None, :, None] >= window_end[:, None, :]).astype(jnp.int32), -1
    )
    windows = jnp.arange(variate_tallies.shape[-1], dtype=jnp.int32)
    picked = jnp.sum(
        jnp.where(
            packed_fragment[:, :, None] == windows[None, None, :], lookback_classes[:, None, :], 0
        ),
        -1,
    )
    return (packed_fragment, picked)


def move(array, axis, pairs):
    return lax.ppermute(array, axis, pairs)


def bits_of(axis, mask):
    place = lax.axis_index(axis)
    index = 0
    for position, m in enumerate(mask):
        index = index + ((place & m) // m) * (1 << position)
    return index


def xor_swap(array, dim, k, plane=None):
    axis, mask = dim
    flip = sum(m for position, m in enumerate(mask) if k >> position & 1)
    size = lax.axis_size(axis)
    if plane is None:
        return lax.ppermute(array, axis, [(i, i ^ flip) for i in range(size)])
    dp = lax.axis_size("dp")
    cells = [c for c in range(lax.axis_size("pipe")) if c // 2 == plane]
    return lax.ppermute(
        array, ("pipe", "dp"), [(c * dp + i, c * dp + (i ^ flip)) for c in cells for i in range(dp)]
    )


def combine_kernel(count, ways, g_ref, *refs):
    ins, outs = refs[:count], refs[count:]
    rows = outs[0].shape[0]
    step = 128 if rows % 128 == 0 else rows
    for k in range(ways):
        base = (g_ref[0] ^ k) * rows
        for r in range(0, rows, step):
            at = pl.ds(pl.multiple_of(base + r, 16), step)
            total = ins[0][at, :].astype(F32)
            for one in ins[1:]:
                total = total + one[at, :].astype(F32)
            outs[k][r : r + step, :] = total.astype(outs[k].dtype)


def combine(arrays, group, ways):
    rows, cols = arrays[0].shape
    return call(
        functools.partial(combine_kernel, len(arrays), ways),
        "s" + "v" * len(arrays),
        [((rows // ways, cols), BF16)] * ways,
        vmem=20 << 20,
        nbytes=rows * cols,
    )(scalars(group), *arrays)


def assemble_kernel(ways, g_ref, *refs):
    out = refs[ways]
    rows = refs[0].shape[0]
    for k in range(ways):
        base = pl.multiple_of((g_ref[0] ^ k) * rows, 16)
        out[pl.ds(base, rows), :] = refs[k][...].astype(out.dtype)


def assemble(arrays, group, dtype=BF16):
    ways = len(arrays)
    rows, cols = arrays[0].shape
    return call(
        functools.partial(assemble_kernel, ways),
        "s" + "v" * ways,
        [((rows * ways, cols), dtype)],
        vmem=20 << 20,
        nbytes=rows * ways * cols,
    )(scalars(group), *arrays)[0]


def dims_of(name):
    if name == "x":
        return [("pipe", (2,))]
    if name == "c":
        return [("pipe", (1,))]
    size = lax.axis_size("dp")
    if name == "y":
        return [("dp", (1,))]
    rest = []
    m = 2
    while m < size:
        rest.append(m)
        m *= 2
    return [("dp", tuple(rest[i : i + 2])) for i in range(0, len(rest), 2)]


def reduce_rows(arrays, order, target=None):
    plane = None
    for name in order:
        if name == "t":
            one = combine(arrays, 0, 1)[0] if len(arrays) > 1 else arrays[0]
            pairs = [(2 * (1 - target) + c, 2 * target + c) for c in range(2)]
            arrays = [one, lax.ppermute(one, "pipe", pairs)]
            plane = target
            continue
        if name == "b":
            one = combine(arrays, 0, 1)[0] if len(arrays) > 1 else arrays[0]
            arrays = [one, xor_swap(one, ("pipe", (2,)), 1)]
            continue
        for dim in dims_of(name):
            ways = 1 << len(dim[1])
            pieces = combine(arrays, bits_of(*dim), ways)
            arrays = [pieces[0]] + [xor_swap(pieces[k], dim, k, plane) for k in range(1, ways)]
    return combine(arrays, 0, 1)[0]


def gather_rows(piece, order, plane=None):
    for name in order:
        for dim in reversed(dims_of(name)):
            ways = 1 << len(dim[1])
            swap_plane = None if name == "x" else plane
            piece = assemble(
                [piece] + [xor_swap(piece, dim, k, swap_plane) for k in range(1, ways)], bits_of(*dim)
            )
    return piece


def all_sum(arrays, order, target=None):
    back = "".join(n for n in reversed(order) if n not in "tb")
    piece = reduce_rows(arrays, order, target)
    return gather_rows(piece, back, None if "x" in order else target)


ORDERS = {"feed1": "tyz", "att1": "yzt", "feed0": "xyz", "att0": "yzt", "shared": "yzb"}


def per_device(
    lookback_readings,
    prediction_adjoint,
    variate_tallies,
    lookback_classes,
    brief_lift_table,
    moderate_lift_table,
    distant_lift_table,
    lift_offsets,
    part_entry_arrays,
    part_shrink_lines,
    part_layernorm_scale,
    part_layernorm_offset,
    mixing_offsets,
    expand_offsets,
    shrink_offsets,
    prediction_matrix,
    prediction_offset,
):
    place = lax.axis_index("pipe")
    core, far = place & 1, place // 2
    tok = lookback_readings[0]
    adjoint = prediction_adjoint[0]
    count = tok.shape[0]
    tables = (brief_lift_table, moderate_lift_table, distant_lift_table)
    entry, shrink = part_entry_arrays[0], part_shrink_lines[0]

    cores = [(0, 1), (1, 0), (2, 3), (3, 2)]
    att_x = move(entry, "pipe", [(0, 2), (2, 0)])
    entry_c = move(entry, "pipe", cores)
    shrink_c = move(shrink, "pipe", cores)
    norm = jnp.concatenate([part_layernorm_scale, part_layernorm_offset], 0)[None]
    norm = assemble_norm(norm, place)
    att_xc = move(att_x, "pipe", [(0, 1), (2, 3)])
    entry_f, att_x = lax.optimization_barrier((entry, att_x))
    up_x = move(entry_f, "pipe", [(1, 3), (3, 1)])
    up_xc = move(up_x, "pipe", [(1, 0), (3, 2)])
    shrink_x = spread(shrink)
    shrink_xc = move(shrink_x, "pipe", cores)
    atts = (entry, entry_c, att_x, att_xc)
    ups = (entry, entry_c, up_x, up_xc)
    downs = (shrink, shrink_c, shrink_x, shrink_xc)

    def att_at(layer):
        return scalars(2 * (far ^ layer) + core, core)

    def feed_at(layer):
        away = 2 * (far ^ layer)
        return scalars(away + 1 - core, away + core, away + 1 - core, core)

    tallies = lax.dynamic_index_in_dim(variate_tallies, place, 0, False)
    classes = lax.dynamic_index_in_dim(lookback_classes, place, 0, False)
    fragment, picked = row_layout(tallies, classes, count)
    segc, segr = fragment.reshape(-1, 1), fragment.reshape(1, -1)
    cls = picked.reshape(-1, 1)

    x0 = embed_fwd(tok, cls, *tables, lift_offsets)
    x1, z0, qkv0, o0, lse0 = attention_fwd(
        att_at(0), atts, x0, mixing_offsets[0], norm[0], segc, segr
    )
    x2, z1, h1, d1 = feed_fwd(
        feed_at(0), ups, downs, x1, expand_offsets[0:1], shrink_offsets[0:1], norm[1]
    )
    x3, z2, qkv2, o2, lse2 = attention_fwd(
        att_at(1), atts, x2, mixing_offsets[1], norm[2], segc, segr
    )
    prediction, gpm, gpb, g, keep3, send3, upb1, vec3 = last_feed(
        feed_at(1), ups, downs, x3, expand_offsets[1:2], shrink_offsets[1:2], norm[3],
        prediction_matrix, prediction_offset[None], adjoint,
    )
    g, keep2, send2, vec2 = attention_bwd(
        att_at(1), atts, g, x2, z2, qkv2, o2, lse2, norm[2], segc, segr
    )
    g, keep1, send1, upb0, vec1 = feed_bwd(feed_at(0), ups, downs, g, x1, z1, h1, d1, norm[1])
    g, keep0, send0, vec0 = attention_bwd(
        att_at(0), atts, g, x0, z0, qkv0, o0, lse0, norm[0], segc, segr
    )
    shared_rows = max(SHARED_ROWS, 32 * lax.axis_size("dp"))
    series, keeps, sends = embed_bwd(
        scalars(core), g, tok, cls, tables, (gpm, gpb, vec0, vec1, vec2, vec3, upb0, upb1), shared_rows
    )

    def chunk(keep, send, name, target):
        return all_sum([keep, move(send, "pipe", cores)], ORDERS[name], target)

    feeds = [chunk(keep1, send1, "feed0", 0), chunk(keep3, send3, "feed1", 1)]
    attns = [chunk(keep0, send0, "att0", 0), chunk(keep2, send2, "att1", 1)]
    feed = jnp.where(far == 0, feeds[0], feeds[1])
    att = jnp.where(far == 0, attns[0], attns[1])
    shared = chunk(keeps, sends, "shared", None)
    shared_other = move(shared, "pipe", cores)
    rows = entry.shape[0] * entry.shape[1] // shrink.shape[1] // 2
    up, down_grad = feed[:rows], feed[rows:].astype(F32)
    up_other = move(up, "pipe", [(0, 1), (2, 3)])
    att_other = move(att, "pipe", [(1, 0), (3, 2)])
    entry_grad = entry_out(scalars(core), att, att_other, up, up_other, entry.shape)
    t0, t1, t2, embb, gain, offset, attb, upb, downb, pw, pb = shared_out(
        scalars(core, place), shared, shared_other, tables, prediction_matrix.shape[1], entry.shape[1]
    )
    return (
        prediction[None],
        series[None],
        t0,
        t1,
        t2,
        embb,
        entry_grad[None],
        down_grad[None],
        gain,
        offset,
        attb,
        upb,
        downb,
        pw,
        pb[0],
    )


def assemble_norm(own, place):
    cores = [(0, 1), (1, 0), (2, 3), (3, 2)]
    other = lax.ppermute(own, "pipe", cores)
    chip = jnp.where(place & 1 == 0, jnp.concatenate([own, other]), jnp.concatenate([other, own]))
    away = xor_swap(chip, ("pipe", (2,)), 1)
    return jnp.where(place // 2 == 0, jnp.concatenate([chip, away]), jnp.concatenate([away, chip]))


def spread(array):
    size = lax.axis_size("dp")
    rows = array.shape[0] // size
    share = lax.dynamic_slice_in_dim(array, bits_over_dp() * rows, rows, 0)
    return gather_rows(xor_swap(share, ("pipe", (2,)), 1), "zy")


def bits_over_dp():
    index = 0
    for name in "yz":
        for dim in dims_of(name):
            index = index * (1 << len(dim[1])) + bits_of(*dim)
    return index


def solution(mesh):
    placed = (
        P("pipe", "dp", None),
        P("pipe", "dp", None),
        P(None, "dp", None),
        P(None, "dp", None),
        P(),
        P(),
        P(),
        P(),
        P("pipe", None, None),
        P("pipe", None, None),
        P("pipe", None),
        P("pipe", None),
        P(),
        P(),
        P(),
        P(),
        P(),
    )
    return jax.shard_map(
        per_device,
        mesh=mesh,
        in_specs=placed,
        out_specs=(
            P("pipe", "dp", None),
            P("pipe", "dp", None),
            P(),
            P(),
            P(),
            P(),
            P("pipe", None, None),
            P("pipe", None, None),
            P("pipe", None),
            P("pipe", None),
            P(),
            P(),
            P(),
            P(),
            P(),
        ),
        check_vma=False,
    )
```

time: 661 us -> 458 us (0.69)
  waiting for transfers between devices: 372 us -> 169 us
  starting transfers between devices: 0.19 us -> 154 us
  matrix products: 114 us -> 0 us
  Pallas kernels: 0 us -> 84.6 us
  blocking collectives: 56 us -> 0 us
  local copies, waits for them, and re-layouts: 67.9 us -> 35.5 us
  other arithmetic: 27.2 us -> 5.27 us
  between operations: 15.4 us -> 2.24 us
    psum x2 -> x0, waiting for transfers between devices: 203 us -> none  [the longest x1 127 us: per_device(): lax.psum((*table_grads, emb_bias, jnp.stack(att_bias), jnp.stack(up_bias)...]
    ppermute x0 -> x68, waiting for transfers between devices: none -> 169 us  [the longest x33 86.7 us: xor_swap(): return lax.ppermute(array, axis, [(i, i ^ flip) for i in range(size)])]
    ppermute x0 -> x68, starting transfers between devices: none -> 154 us  [the longest x33 72.6 us: xor_swap(): return lax.ppermute(array, axis, [(i, i ^ flip) for i in range(size)])]
    dot_general x46 -> x0, matrix products: 100 us -> none  [the longest x2 24.2 us: feed_forward(): jnp.dot(inputs_bf, up_matrix, preferred_element_type=jnp.float32)]
    reduce_scatter x1 -> x0, waiting for transfers between devices: 95.7 us -> none  [per_device(): big = lax.psum_scatter(big, 'pipe', scatter_dimension=0, tiled=True)[0]]
    pallas_call x0 -> x44, Pallas kernels: none -> 84.6 us  [run(): pl.pallas_call(kernel, out_shape=[jax.ShapeDtypeStruct(s, d) for s, d in...]
    all_gather x2 -> x0, waiting for transfers between devices: 72.2 us -> none  [the longest x1 55.4 us: per_device(): lax.all_gather(part_entry_arrays, 'pipe', axis=0, tiled=True)]
    psum x1 -> x0, blocking collectives: 44.5 us -> none  [per_device(): lax.psum((*table_grads, emb_bias, jnp.stack(att_bias), jnp.stack(up_bias)...]
  transfers between devices with their start and end apart: 5 -> 68, of which waited for: 5 -> 25; matrix products, arithmetic and copies ran while one was open for 6% -> 5% of each run, Pallas kernels for 0% -> 11%
where the time goes in v2:
time: 458 us; the launch traced here: 450 us
  waiting for transfers between devices  169 us (37%)
  starting transfers between devices  154 us (34%)
  Pallas kernels  84.6 us (18%)
  local copies, waits for them, and re-layouts  35.5 us (8%)
  other arithmetic  5.27 us (1%)
    ppermute x33, waiting for transfers between devices, xor_swap(): return lax.ppermute(array, axis, [(i, i ^ flip) for i in range(size)])  86.7 us
    pallas_call x44, Pallas kernels, run(): pl.pallas_call(kernel, out_shape=[jax.ShapeDtypeStruct(s, d) for s, d in...  84.6 us
    ppermute x33, starting transfers between devices, xor_swap(): return lax.ppermute(array, axis, [(i, i ^ flip) for i in range(size)])  72.6 us
    ppermute x15, waiting for transfers between devices, move(): return lax.ppermute(array, axis, pairs)  45.7 us
    ppermute x3, starting transfers between devices, reduce_rows(): arrays = [one, lax.ppermute(one, 'pipe', pairs)]  38.3 us
    unnamed x127, local copies, waits for them, and re-layouts  30.9 us
    ppermute x3, waiting for transfers between devices, reduce_rows(): arrays = [one, lax.ppermute(one, 'pipe', pairs)]  27.6 us
    ppermute x16, starting transfers between devices, xor_swap(): lax.ppermute(array, ('pipe', 'dp'), [(c * dp + i, c * dp + (i ^ flip)) fo...  22 us
  transfers between devices with their start and end apart: 68, of which 25 were waited for; matrix products, arithmetic and copies ran while one was open for 5% of the time, Pallas kernels for 11%

profile of v2, /device:TPU:0, one launch (start us, length us, event | category | flops | bytes accessed | tf_op | source)
XLA Modules:
  0.0 450.4 jit_solution(17163966116362041998)
XLA Ops:
  0.7 5.0 %collective-permute-start.1 = (bf16[512,2048]{1,0:T(8,128)(2,1)}, bf16[512,2048]{1,0:T(8,128)(2,1)}, u32[]{:S(2)}, u32[]{:S(2)}) collective-permute-start(bf16[512,2048]{1,0:T(8,128)(2,1)} %bitcast.65), channel_id=1, source_target_pairs={{0,16},{16,0},{1,17},{17,1},{2,18},{18,2},{3,19},{19,3},{4,20},{20... | collective-permute-start | bytes 6291464 | tf_op jit(solution)/shard_map/ppermute | solution.py:548
  5.7 45.6 %collective-permute-done.1.w2 = bf16[512,2048]{1,0:T(8,128)(2,1)} collective-permute-done((bf16[512,2048]{1,0:T(8,128)(2,1)}, bf16[512,2048]{1,0:T(8,128)(2,1)}, u32[]{:S(2)}, u32[]{:S(2)}) %collective-permute-start.1) | collective-permute-done | bytes 2097184 | tf_op jit(solution)/shard_map/ppermute | solution.py:548
  56.7 3.5 collective-permute-start.11
  72.5 5.7 %collective-permute-done.7.refs_2_ = bf16[128,512]{1,0:T(8,128)(2,1)S(1)} collective-permute-done((bf16[128,512]{1,0:T(8,128)(2,1)S(1)}, bf16[128,512]{1,0:T(8,128)(2,1)S(1)}, u32[]{:S(2)}, u32[]{:S(2)}) %collective-permute-start.7) | collective-permute-done | bytes 131104 | tf_op jit(solution)/shard_map/ppermute | solution.py:564
  86.6 6.0 %collective-permute-done.9.refs_1_ = bf16[512,512]{1,0:T(8,128)(2,1)S(1)} collective-permute-done((bf16[512,512]{1,0:T(8,128)(2,1)S(1)}, bf16[512,512]{1,0:T(8,128)(2,1)S(1)}, u32[]{:S(2)}, u32[]{:S(2)}) %collective-permute-start.9) | collective-permute-done | bytes 524320 | tf_op jit(solution)/shard_map/ppermute | solution.py:564
  101.8 6.6 %shard_map.283 = (bf16[512,512]{1,0:T(8,128)(2,1)S(1)}, f32[512,512]{1,0:T(8,128)S(1)}, bf16[512,1536]{1,0:T(8,128)(2,1)S(1)}, bf16[512,512]{1,0:T(8,128)(2,1)S(1)}, f32[8,512]{1,0:T(8,128)S(1)}) custom-call(s32[2]{0:T(128)S(1)} %copy-done.15, bf16[512,2048]{1,0:T(8,128)(2,1)S(1)} %bitcast.68, bf16[512,2048]{1,0:T(8,128)(2,1)} %collective-permute-done.w1.u1, ...), custom_call_target="tpu_custom_call" | custom-call | flops 5000000000 | tf_op jit(solution)/shard_map/pallas_call | solution.py:401
  110.7 8.1 %shard_map.284 = (bf16[512,512]{1,0:T(8,128)(2,1)S(1)}, f32[512,512]{1,0:T(8,128)S(1)}, bf16[512,2048]{1,0:T(8,128)(2,1)S(1)}, bf16[512,2048]{1,0:T(8,128)(2,1)S(1)}) custom-call(s32[4]{0:T(128)S(1)} %get-tuple-element.239.at_ref, bf16[512,2048]{1,0:T(8,128)(2,1)S(1)} %bitcast.69, bf16[512,2048]{1,0:T(8,128)(2,1)} %collective-permute-done.w1.u1, ...), custom_call_target="tpu_custom_call" | custom-call | flops 5000000000 | tf_op jit(solution)/shard_map/pallas_call | solution.py:401
  120.2 8.0 %shard_map.285 = (bf16[512,512]{1,0:T(8,128)(2,1)S(1)}, f32[512,512]{1,0:T(8,128)S(1)}, bf16[512,1536]{1,0:T(8,128)(2,1)S(1)}, bf16[512,512]{1,0:T(8,128)(2,1)S(1)}, f32[8,512]{1,0:T(8,128)S(1)}) custom-call(s32[2]{0:T(128)S(1)} %copy-done.17, bf16[512,2048]{1,0:T(8,128)(2,1)S(1)} %bitcast.70, bf16[512,2048]{1,0:T(8,128)(2,1)} %collective-permute-done.w1.u1, ...), custom_call_target="tpu_custom_call" | custom-call | flops 5000000000 | tf_op jit(solution)/shard_map/pallas_call | solution.py:401
  128.2 13.3 %shard_map.286 = (bf16[512,96]{1,0:T(8,128)(2,1)S(1)}, f32[96,512]{1,0:T(8,128)S(1)}, f32[1,96]{1,0:T(1,128)S(1)}, bf16[512,512]{1,0:T(8,128)(2,1)S(1)}, bf16[20...) custom-call(s32[4]{0:T(128)S(1)} %get-tuple-element.238.at_ref, ...), custom_call_target="tpu_custom_call" | custom-call | flops 8000000000 | tf_op jit(solution)/shard_map/pallas_call | solution.py:401
  143.4 12.0 %shard_map.287 = (bf16[512,512]{1,0:T(8,128)(2,1)S(1)}, bf16[1024,512]{1,0:T(8,128)(2,1)S(1)}, bf16[1024,512]{1,0:T(8,128)(2,1)S(1)}, f32[5,512]{1,0:T(8,128)S(1)}) custom-call(s32[2]{0:T(128)S(1)} %copy-done.17, bf16[512,2048]{1,0:T(8,128)(2,1)S(1)} %bitcast.72, bf16[512,2048]{1,0:T(8,128)(2,1)} %collective-permute-done.w1.u1, ...), custom_call_target="tpu_custom_call" | custom-call | flops 7000000000 | tf_op jit(solution)/shard_map/pallas_call | solution.py:401
  156.3 10.0 %shard_map.288 = (bf16[512,512]{1,0:T(8,128)(2,1)S(1)}, bf16[2048,512]{1,0:T(8,128)(2,1)S(1)}, bf16[2048,512]{1,0:T(8,128)(2,1)}, f32[4,512]{1,0:T(4,128)S(1)}, f32[3,512]{1,0:T(4,128)S(1)}) custom-call(s32[4]{0:T(128)S(1)} %get-tuple-element.239.at_ref, bf16[512,2048]{1,0:T(8,128)(2,1)S(1)} %bitcast.73, bf16[512,2048]{1,0:T(8,128)(2,1)} %collective-permute-done.w1.u1, ...), custom_call_target="tpu_custom_call" | custom-call | flops 6000000000 | tf_op jit(solution)/shard_map/pallas_call | solution.py:401
  168.4 4.0 collective-permute-start.58
  180.0 10.5 %shard_map.289 = (bf16[512,512]{1,0:T(8,128)(2,1)S(1)}, bf16[1024,512]{1,0:T(8,128)(2,1)S(1)}, bf16[1024,512]{1,0:T(8,128)(2,1)S(1)}, f32[5,512]{1,0:T(8,128)S(1)}) custom-call(s32[2]{0:T(128)S(1)} %copy-done.16, bf16[512,2048]{1,0:T(8,128)(2,1)S(1)} %bitcast.74, bf16[512,2048]{1,0:T(8,128)(2,1)} %collective-permute-done.w1.u1, ...), custom_call_target="tpu_custom_call" | custom-call | flops 7000000000 | tf_op jit(solution)/shard_map/pallas_call | solution.py:401
  191.8 25.2 %collective-permute-done.58.refs_1_ = bf16[2048,512]{1,0:T(8,128)(2,1)} collective-permute-done((bf16[2048,512]{1,0:T(8,128)(2,1)S(1)}, bf16[2048,512]{1,0:T(8,128)(2,1)}, u32[]{:S(2)}, u32[]{:S(2)}) %collective-permute-start.58) | collective-permute-done | bytes 2097184 | tf_op jit(solution)/shard_map/ppermute | solution.py:639
  219.8 19.7 %collective-permute-done.47.refs_1_ = bf16[1024,512]{1,0:T(8,128)(2,1)S(1)} collective-permute-done((bf16[1024,512]{1,0:T(8,128)(2,1)S(1)}, bf16[1024,512]{1,0:T(8,128)(2,1)S(1)}, u32[]{:S(2)}, u32[]{:S(2)}) %collective-permute-start.47) | collective-permute-done | bytes 1048608 | tf_op jit(solution)/shard_map/ppermute | solution.py:564
  243.9 10.6 %collective-permute-done.48.refs_1_ = bf16[512,512]{1,0:T(8,128)(2,1)S(1)} collective-permute-done((bf16[512,512]{1,0:T(8,128)(2,1)S(1)}, bf16[512,512]{1,0:T(8,128)(2,1)S(1)}, u32[]{:S(2)}, u32[]{:S(2)}) %collective-permute-start.48) | collective-permute-done | bytes 524320 | tf_op jit(solution)/shard_map/ppermute | solution.py:564
  254.7 3.0 collective-permute-start.49
  258.8 3.2 collective-permute-done.49.refs_1_
  263.4 5.7 %collective-permute-done.50.refs_2_ = bf16[128,512]{1,0:T(8,128)(2,1)S(1)} collective-permute-done((bf16[128,512]{1,0:T(8,128)(2,1)S(1)}, bf16[128,512]{1,0:T(8,128)(2,1)S(1)}, u32[]{:S(2)}, u32[]{:S(2)}) %collective-permute-start.50) | collective-permute-done | bytes 131104 | tf_op jit(solution)/shard_map/ppermute | solution.py:564
  277.5 5.6 %collective-permute-done.53.refs_2_ = bf16[128,512]{1,0:T(8,128)(2,1)S(1)} collective-permute-done((bf16[128,512]{1,0:T(8,128)(2,1)S(1)}, bf16[128,512]{1,0:T(8,128)(2,1)S(1)}, u32[]{:S(2)}, u32[]{:S(2)}) %collective-permute-start.53) | collective-permute-done | bytes 131104 | tf_op jit(solution)/shard_map/ppermute | solution.py:564
  287.9 4.7 %collective-permute-done.38.refs_2_ = bf16[128,512]{1,0:T(8,128)(2,1)S(1)} collective-permute-done((bf16[128,512]{1,0:T(8,128)(2,1)S(1)}, bf16[128,512]{1,0:T(8,128)(2,1)S(1)}, u32[]{:S(2)}, u32[]{:S(2)}) %collective-permute-start.38) | collective-permute-done | bytes 131104 | tf_op jit(solution)/shard_map/ppermute | solution.py:564
  303.6 4.1 collective-permute-done.28.refs_2_
  308.4 33.0 %collective-permute-start.40 = (bf16[128,512]{1,0:T(8,128)(2,1)S(1)}, bf16[128,512]{1,0:T(8,128)(2,1)S(1)}, u32[]{:S(2)}, u32[]{:S(2)}) collective-permute-start(bf16[128,512]{1,0:T(8,128)(2,1)S(1)} %shard_map.306.refs_0_), channel_id=1, source_target_pairs={{0,16},{8,24},{1,17},{9,25},{2,18},{10,26},{3,19},{11,27},{4,20},{... | collective-permute-start | bytes 393224 | tf_op jit(solution)/shard_map/ppermute | solution.py:639
  347.5 17.7 %collective-permute-start.56 = (bf16[1024,512]{1,0:T(8,128)(2,1)S(1)}, bf16[1024,512]{1,0:T(8,128)(2,1)S(1)}, u32[]{:S(2)}, u32[]{:S(2)}) collective-permute-start(bf16[1024,512]{1,0:T(8,128)(2,1)S(1)} %shard_map.315.refs_0_), channel_id=1, source_target_pairs={{0,16},{8,24},{16,0},{24,8},{1,17},{9,25},{17,1},{25,9},{2,18},{10... | collective-permute-start | bytes 3145736 | tf_op jit(solution)/shard_map/ppermute | solution.py:564
  371.9 4.3 collective-permute-start.33
  380.7 3.4 collective-permute-start.34
  386.3 5.5 %collective-permute-done.34.refs_1_ = bf16[512,512]{1,0:T(8,128)(2,1)S(1)} collective-permute-done((bf16[512,512]{1,0:T(8,128)(2,1)S(1)}, bf16[512,512]{1,0:T(8,128)(2,1)S(1)}, u32[]{:S(2)}, u32[]{:S(2)}) %collective-permute-start.34) | collective-permute-done | bytes 524320 | tf_op jit(solution)/shard_map/ppermute | solution.py:567
  395.5 4.1 collective-permute-start.67
  401.2 4.2 collective-permute-done.15.refs_1_
  414.4 5.5 %collective-permute-start.19 = (bf16[48,512]{1,0:T(8,128)(2,1)S(1)}, bf16[48,512]{1,0:T(8,128)(2,1)S(1)}, u32[]{:S(2)}, u32[]{:S(2)}) collective-permute-start(bf16[48,512]{1,0:T(8,128)(2,1)S(1)} %shard_map.293.refs_0_), channel_id=1, source_target_pairs={{0,16},{8,24},{16,0},{24,8},{1,17},{9,25},{17,1},{25,9},{2,18},{10... | collective-permute-start | bytes 147464 | tf_op jit(solution)/shard_map/ppermute | solution.py:564
  431.6 4.2 collective-permute-done.23.refs_1_
  446.4 3.5 shard_map.323
  (296 shorter events, 143.0 us)
Async XLA Ops:
  0.7 50.6 %collective-permute-start.1 = (bf16[512,2048]{1,0:T(8,128)(2,1)}, bf16[512,2048]{1,0:T(8,128)(2,1)}, u32[]{:S(2)}, u32[]{:S(2)}) collective-permute-start(bf16[512,2048]{1,0:T(8,128)(2,1)} %bitcast.65), channel_id=1, source_target_pairs={{0,16},{16,0},{1,17},{17,1},{2,18},{18,2},{3,19},{19,3},{4,20},{20... | collective-permute-start | bytes 6291464 | tf_op jit(solution)/shard_map/ppermute | solution.py:548
  53.4 45.1 %collective-permute-start = (bf16[512,2048]{1,0:T(8,128)(2,1)}, bf16[512,2048]{1,0:T(8,128)(2,1)}, u32[]{:S(2)}, u32[]{:S(2)}) collective-permute-start(bf16[512,2048]{1,0:T(8,128)(2,1)} %bitcast.67), channel_id=1, source_target_pairs={{0,8},{8,0},{16,24},{24,16},{1,9},{9,1},{17,25},{25,17},{2,10},{10... | collective-permute-start | bytes 6291464 | tf_op jit(solution)/shard_map/ppermute | solution.py:548
  56.7 41.8 %collective-permute-start.11 = (bf16[512,2048]{1,0:T(8,128)(2,1)}, bf16[512,2048]{1,0:T(8,128)(2,1)}, u32[]{:S(2)}, u32[]{:S(2)}) collective-permute-start(bf16[512,2048]{1,0:T(8,128)(2,1)} %collective-permute-done.1.w2), channel_id=1, source_target_pairs={{0,8},{16,24},{1,9},{17,25},{2,10},{18,26},{3,11},{19,27},{4,12},{... | collective-permute-start | bytes 6291464 | tf_op jit(solution)/shard_map/ppermute | solution.py:548
  63.2 47.5 %collective-permute-start.3 = (bf16[512,2048]{1,0:T(8,128)(2,1)}, bf16[512,2048]{1,0:T(8,128)(2,1)}, u32[]{:S(2)}, u32[]{:S(2)}) collective-permute-start(bf16[512,2048]{1,0:T(8,128)(2,1)} %collective-permute-done.2.u2), channel_id=1, source_target_pairs={{8,0},{24,16},{9,1},{25,17},{10,2},{26,18},{11,3},{27,19},{12,4},{... | collective-permute-start | bytes 6291464 | tf_op jit(solution)/shard_map/ppermute | solution.py:548
  78.3 14.3 %collective-permute-start.9 = (bf16[512,512]{1,0:T(8,128)(2,1)S(1)}, bf16[512,512]{1,0:T(8,128)(2,1)S(1)}, u32[]{:S(2)}, u32[]{:S(2)}) collective-permute-start(bf16[512,512]{1,0:T(8,128)(2,1)S(1)} %shard_map.280.refs_0_), channel_id=1, source_target_pairs={{0,1},{1,0},{2,3},{3,2},{4,5},{5,4},{6,7},{7,6},{8,9},{9,8},{10,11... | collective-permute-start | bytes 1572872 | tf_op jit(solution)/shard_map/ppermute | solution.py:564
  92.6 18.1 %collective-permute-start.4 = (bf16[1024,512]{1,0:T(8,128)(2,1)S(1)}, bf16[1024,512]{1,0:T(8,128)(2,1)}, u32[]{:S(2)}, u32[]{:S(2)}) collective-permute-start(bf16[1024,512]{1,0:T(8,128)(2,1)S(1)} %bitcast.59), channel_id=1, source_target_pairs={{0,8},{8,0},{16,24},{24,16},{1,9},{9,1},{17,25},{25,17},{2,10},{10... | collective-permute-start | bytes 3145736 | tf_op jit(solution)/shard_map/ppermute | solution.py:548
  92.7 18.0 %collective-permute-start.10 = (bf16[1024,512]{1,0:T(8,128)(2,1)S(1)}, bf16[1024,512]{1,0:T(8,128)(2,1)}, u32[]{:S(2)}, u32[]{:S(2)}) collective-permute-start(bf16[1024,512]{1,0:T(8,128)(2,1)S(1)} %shard_map.281.d2), channel_id=1, source_target_pairs={{0,8},{8,0},{16,24},{24,16},{1,9},{9,1},{17,25},{25,17},{2,10},{10... | collective-permute-start | bytes 3145736 | tf_op jit(solution)/shard_map/ppermute | solution.py:548
  142.7 24.3 %collective-permute-start.57 = (bf16[2048,512]{1,0:T(8,128)(2,1)S(1)}, bf16[2048,512]{1,0:T(8,128)(2,1)S(1)}, u32[]{:S(2)}, u32[]{:S(2)}) collective-permute-start(bf16[2048,512]{1,0:T(8,128)(2,1)S(1)} %get-tuple-element.167), channel_id=1, source_target_pairs={{0,8},{8,0},{16,24},{24,16},{1,9},{9,1},{17,25},{25,17},{2,10},{10... | collective-permute-start | bytes 6291464 | tf_op jit(solution)/shard_map/ppermute | solution.py:548
  168.4 48.6 %collective-permute-start.58 = (bf16[2048,512]{1,0:T(8,128)(2,1)S(1)}, bf16[2048,512]{1,0:T(8,128)(2,1)}, u32[]{:S(2)}, u32[]{:S(2)}) collective-permute-start(bf16[2048,512]{1,0:T(8,128)(2,1)S(1)} %shard_map.317.refs_0_), channel_id=1, source_target_pairs={{0,16},{8,24},{1,17},{9,25},{2,18},{10,26},{3,19},{11,27},{4,20},{... | collective-permute-start | bytes 6291464 | tf_op jit(solution)/shard_map/ppermute | solution.py:639
  172.4 68.9 %collective-permute-start.35 = (bf16[1024,512]{1,0:T(8,128)(2,1)}, bf16[1024,512]{1,0:T(8,128)(2,1)S(1)}, u32[]{:S(2)}, u32[]{:S(2)}) collective-permute-start(bf16[1024,512]{1,0:T(8,128)(2,1)} %copy-done.21), channel_id=1, source_target_pairs={{0,8},{8,0},{16,24},{24,16},{1,9},{9,1},{17,25},{25,17},{2,10},{10... | collective-permute-start | bytes 3145736 | tf_op jit(solution)/shard_map/ppermute | solution.py:548
  176.9 62.6 %collective-permute-start.47 = (bf16[1024,512]{1,0:T(8,128)(2,1)S(1)}, bf16[1024,512]{1,0:T(8,128)(2,1)S(1)}, u32[]{:S(2)}, u32[]{:S(2)}) collective-permute-start(bf16[1024,512]{1,0:T(8,128)(2,1)S(1)} %get-tuple-element.159), channel_id=1, source_target_pairs={{0,16},{8,24},{16,0},{24,8},{1,17},{9,25},{17,1},{25,9},{2,18},{10... | collective-permute-start | bytes 3145736 | tf_op jit(solution)/shard_map/ppermute | solution.py:564
  190.5 51.7 %collective-permute-start.25 = (bf16[1024,512]{1,0:T(8,128)(2,1)S(1)}, bf16[1024,512]{1,0:T(8,128)(2,1)S(1)}, u32[]{:S(2)}, u32[]{:S(2)}) collective-permute-start(bf16[1024,512]{1,0:T(8,128)(2,1)S(1)} %get-tuple-element.141), channel_id=1, source_target_pairs={{0,8},{8,0},{16,24},{24,16},{1,9},{9,1},{17,25},{25,17},{2,10},{10... | collective-permute-start | bytes 3145736 | tf_op jit(solution)/shard_map/ppermute | solution.py:548
  219.1 54.9 %collective-permute-start.59 = (bf16[1024,512]{1,0:T(8,128)(2,1)S(1)}, bf16[1024,512]{1,0:T(8,128)(2,1)S(1)}, u32[]{:S(2)}, u32[]{:S(2)}) collective-permute-start(bf16[1024,512]{1,0:T(8,128)(2,1)S(1)} %get-tuple-element.169), channel_id=1, source_target_pairs={{16,17},{17,16},{18,19},{19,18},{20,21},{21,20},{22,23},{23,22},{2... | collective-permute-start | bytes 3145736 | tf_op jit(solution)/shard_map/ppermute | solution.py:567
  239.7 14.8 %collective-permute-start.48 = (bf16[512,512]{1,0:T(8,128)(2,1)S(1)}, bf16[512,512]{1,0:T(8,128)(2,1)S(1)}, u32[]{:S(2)}, u32[]{:S(2)}) collective-permute-start(bf16[512,512]{1,0:T(8,128)(2,1)S(1)} %get-tuple-element.161), channel_id=1, source_target_pairs={{0,1},{1,0},{2,3},{3,2},{4,5},{5,4},{6,7},{7,6},{8,9},{9,8},{10,11... | collective-permute-start | bytes 1572872 | tf_op jit(solution)/shard_map/ppermute | solution.py:564
  241.5 30.8 %collective-permute-start.36 = (bf16[512,512]{1,0:T(8,128)(2,1)S(1)}, bf16[512,512]{1,0:T(8,128)(2,1)S(1)}, u32[]{:S(2)}, u32[]{:S(2)}) collective-permute-start(bf16[512,512]{1,0:T(8,128)(2,1)S(1)} %get-tuple-element.151), channel_id=1, source_target_pairs={{0,1},{1,0},{2,3},{3,2},{4,5},{5,4},{6,7},{7,6},{8,9},{9,8},{10,11... | collective-permute-start | bytes 1572872 | tf_op jit(solution)/shard_map/ppermute | solution.py:564
  242.4 33.8 %collective-permute-start.26 = (bf16[512,512]{1,0:T(8,128)(2,1)S(1)}, bf16[512,512]{1,0:T(8,128)(2,1)S(1)}, u32[]{:S(2)}, u32[]{:S(2)}) collective-permute-start(bf16[512,512]{1,0:T(8,128)(2,1)S(1)} %get-tuple-element.143), channel_id=1, source_target_pairs={{0,1},{1,0},{2,3},{3,2},{4,5},{5,4},{6,7},{7,6},{8,9},{9,8},{10,11... | collective-permute-start | bytes 1572872 | tf_op jit(solution)/shard_map/ppermute | solution.py:564
  276.2 19.4 %collective-permute-start.60 = (bf16[256,512]{1,0:T(8,128)(2,1)S(1)}, bf16[256,512]{1,0:T(8,128)(2,1)S(1)}, u32[]{:S(2)}, u32[]{:S(2)}) collective-permute-start(bf16[256,512]{1,0:T(8,128)(2,1)S(1)} %get-tuple-element.171), channel_id=1, source_target_pairs={{16,18},{17,19},{18,16},{19,17},{20,22},{21,23},{22,20},{23,21},{2... | collective-permute-start | bytes 786440 | tf_op jit(solution)/shard_map/ppermute | solution.py:567
  276.8 18.7 %collective-permute-start.61 = (bf16[256,512]{1,0:T(8,128)(2,1)S(1)}, bf16[256,512]{1,0:T(8,128)(2,1)S(1)}, u32[]{:S(2)}, u32[]{:S(2)}) collective-permute-start(bf16[256,512]{1,0:T(8,128)(2,1)S(1)} %get-tuple-element.172), channel_id=1, source_target_pairs={{16,20},{17,21},{18,22},{19,23},{20,16},{21,17},{22,18},{23,19},{2... | collective-permute-start | bytes 786440 | tf_op jit(solution)/shard_map/ppermute | solution.py:567
  283.2 13.7 %collective-permute-start.62 = (bf16[256,512]{1,0:T(8,128)(2,1)S(1)}, bf16[256,512]{1,0:T(8,128)(2,1)S(1)}, u32[]{:S(2)}, u32[]{:S(2)}) collective-permute-start(bf16[256,512]{1,0:T(8,128)(2,1)S(1)} %get-tuple-element.173), channel_id=1, source_target_pairs={{16,22},{17,23},{18,20},{19,21},{20,18},{21,19},{22,16},{23,17},{2... | collective-permute-start | bytes 786440 | tf_op jit(solution)/shard_map/ppermute | solution.py:567
  286.1 59.1 %collective-permute-start.55 = (bf16[512,512]{1,0:T(8,128)(2,1)S(1)}, bf16[512,512]{1,0:T(8,128)(2,1)S(1)}, u32[]{:S(2)}, u32[]{:S(2)}) collective-permute-start(bf16[512,512]{1,0:T(8,128)(2,1)S(1)} %shard_map.314.refs_0_), channel_id=1, source_target_pairs={{0,1},{1,0},{2,3},{3,2},{4,5},{5,4},{6,7},{7,6},{8,9},{9,8},{10,11... | collective-permute-start | bytes 1572872 | tf_op jit(solution)/shard_map/ppermute | solution.py:564
  300.9 45.0 %collective-permute-start.63 = (bf16[256,512]{1,0:T(8,128)(2,1)S(1)}, bf16[256,512]{1,0:T(8,128)(2,1)S(1)}, u32[]{:S(2)}, u32[]{:S(2)}) collective-permute-start(bf16[256,512]{1,0:T(8,128)(2,1)S(1)} %shard_map.320.refs_0_), channel_id=1, source_target_pairs={{16,18},{17,19},{18,16},{19,17},{20,22},{21,23},{22,20},{23,21},{2... | collective-permute-start | bytes 786440 | tf_op jit(solution)/shard_map/ppermute | solution.py:567
  302.9 43.7 %collective-permute-start.64 = (bf16[256,512]{1,0:T(8,128)(2,1)S(1)}, bf16[256,512]{1,0:T(8,128)(2,1)S(1)}, u32[]{:S(2)}, u32[]{:S(2)}) collective-permute-start(bf16[256,512]{1,0:T(8,128)(2,1)S(1)} %shard_map.320.refs_0_), channel_id=1, source_target_pairs={{16,20},{17,21},{18,22},{19,23},{20,16},{21,17},{22,18},{23,19},{2... | collective-permute-start | bytes 786440 | tf_op jit(solution)/shard_map/ppermute | solution.py:567
  307.7 39.8 %collective-permute-start.65 = (bf16[256,512]{1,0:T(8,128)(2,1)S(1)}, bf16[256,512]{1,0:T(8,128)(2,1)S(1)}, u32[]{:S(2)}, u32[]{:S(2)}) collective-permute-start(bf16[256,512]{1,0:T(8,128)(2,1)S(1)} %shard_map.320.refs_0_), channel_id=1, source_target_pairs={{16,22},{17,23},{18,20},{19,21},{20,18},{21,19},{22,16},{23,17},{2... | collective-permute-start | bytes 786440 | tf_op jit(solution)/shard_map/ppermute | solution.py:567
  308.4 35.5 %collective-permute-start.40 = (bf16[128,512]{1,0:T(8,128)(2,1)S(1)}, bf16[128,512]{1,0:T(8,128)(2,1)S(1)}, u32[]{:S(2)}, u32[]{:S(2)}) collective-permute-start(bf16[128,512]{1,0:T(8,128)(2,1)S(1)} %shard_map.306.refs_0_), channel_id=1, source_target_pairs={{0,16},{8,24},{1,17},{9,25},{2,18},{10,26},{3,19},{11,27},{4,20},{... | collective-permute-start | bytes 393224 | tf_op jit(solution)/shard_map/ppermute | solution.py:639
  343.9 21.4 %collective-permute-start.30 = (bf16[128,512]{1,0:T(8,128)(2,1)S(1)}, bf16[128,512]{1,0:T(8,128)(2,1)S(1)}, u32[]{:S(2)}, u32[]{:S(2)}) collective-permute-start(bf16[128,512]{1,0:T(8,128)(2,1)S(1)} %shard_map.300.refs_0_), channel_id=1, source_target_pairs={{16,0},{24,8},{17,1},{25,9},{18,2},{26,10},{19,3},{27,11},{20,4},{... | collective-permute-start | bytes 393224 | tf_op jit(solution)/shard_map/ppermute | solution.py:639
  345.2 20.8 %collective-permute-start.41 = (bf16[128,512]{1,0:T(8,128)(2,1)S(1)}, bf16[128,512]{1,0:T(8,128)(2,1)S(1)}, u32[]{:S(2)}, u32[]{:S(2)}) collective-permute-start(bf16[128,512]{1,0:T(8,128)(2,1)S(1)} %shard_map.307.refs_0_), channel_id=1, source_target_pairs={{16,18},{17,19},{18,16},{19,17},{20,22},{21,23},{22,20},{23,21},{2... | collective-permute-start | bytes 393224 | tf_op jit(solution)/shard_map/ppermute | solution.py:567
  345.9 23.2 %collective-permute-start.42 = (bf16[128,512]{1,0:T(8,128)(2,1)S(1)}, bf16[128,512]{1,0:T(8,128)(2,1)S(1)}, u32[]{:S(2)}, u32[]{:S(2)}) collective-permute-start(bf16[128,512]{1,0:T(8,128)(2,1)S(1)} %shard_map.307.refs_0_), channel_id=1, source_target_pairs={{16,20},{17,21},{18,22},{19,23},{20,16},{21,17},{22,18},{23,19},{2... | collective-permute-start | bytes 393224 | tf_op jit(solution)/shard_map/ppermute | solution.py:567
  346.6 25.3 %collective-permute-start.43 = (bf16[128,512]{1,0:T(8,128)(2,1)S(1)}, bf16[128,512]{1,0:T(8,128)(2,1)S(1)}, u32[]{:S(2)}, u32[]{:S(2)}) collective-permute-start(bf16[128,512]{1,0:T(8,128)(2,1)S(1)} %shard_map.307.refs_0_), channel_id=1, source_target_pairs={{16,22},{17,23},{18,20},{19,21},{20,18},{21,19},{22,16},{23,17},{2... | collective-permute-start | bytes 393224 | tf_op jit(solution)/shard_map/ppermute | solution.py:567
  347.5 45.8 %collective-permute-start.56 = (bf16[1024,512]{1,0:T(8,128)(2,1)S(1)}, bf16[1024,512]{1,0:T(8,128)(2,1)S(1)}, u32[]{:S(2)}, u32[]{:S(2)}) collective-permute-start(bf16[1024,512]{1,0:T(8,128)(2,1)S(1)} %shard_map.315.refs_0_), channel_id=1, source_target_pairs={{0,16},{8,24},{16,0},{24,8},{1,17},{9,25},{17,1},{25,9},{2,18},{10... | collective-permute-start | bytes 3145736 | tf_op jit(solution)/shard_map/ppermute | solution.py:564
  365.2 28.2 %collective-permute-start.66 = (bf16[1024,512]{1,0:T(8,128)(2,1)S(1)}, bf16[1024,512]{1,0:T(8,128)(2,1)S(1)}, u32[]{:S(2)}, u32[]{:S(2)}) collective-permute-start(bf16[1024,512]{1,0:T(8,128)(2,1)S(1)} %shard_map.321.refs_0_), channel_id=1, source_target_pairs={{16,17},{17,16},{18,19},{19,18},{20,21},{21,20},{22,23},{23,22},{2... | collective-permute-start | bytes 3145736 | tf_op jit(solution)/shard_map/ppermute | solution.py:567
  392.0 54.4 %collective-permute-start.45 = (bf16[1024,512]{1,0:T(8,128)(2,1)S(1)}, bf16[1024,512]{1,0:T(8,128)(2,1)S(1)}, u32[]{:S(2)}, u32[]{:S(2)}) collective-permute-start(bf16[1024,512]{1,0:T(8,128)(2,1)S(1)} %broadcast_select_fusion.1.att_ref), channel_id=1, source_target_pairs={{8,0},{24,16},{9,1},{25,17},{10,2},{26,18},{11,3},{27,19},{12,4},{... | collective-permute-start | bytes 3145736 | tf_op jit(solution)/shard_map/ppermute | solution.py:548
  395.5 50.9 %collective-permute-start.67 = (bf16[1024,512]{1,0:T(8,128)(2,1)S(1)}, bf16[1024,512]{1,0:T(8,128)(2,1)}, u32[]{:S(2)}, u32[]{:S(2)}) collective-permute-start(bf16[1024,512]{1,0:T(8,128)(2,1)S(1)} %get-tuple-element.227.up_ref), channel_id=1, source_target_pairs={{0,8},{16,24},{1,9},{17,25},{2,10},{18,26},{3,11},{19,27},{4,12},{... | collective-permute-start | bytes 3145736 | tf_op jit(solution)/shard_map/ppermute | solution.py:548
  (95 other events, 1231.6 us)
